TPU v7x, 128 devices: a whole 4x4x4 slice. The times are simulated.
128 devices in a mesh: grp: 4 (over y), inner: 32 (over z, x, core).
Axes of the slice: x: 4, y: 4, z: 4, core: 2. Of those that a mesh axis runs over, the one named last changes fastest.
Arguments:
- amplitude: float32 [1024, 16384], P(('grp', 'inner')), may hold values from -6 to 6
- integrals: float32 [16384, 128, 128], P(('grp', 'inner')), may hold values from -0.09375 to 0.09375
- tile_owner: int32 [16384, 1], P(('grp', 'inner')), may hold values from 0 to 127; in each aligned block of 128 rows (0 to 127, 128 to 255, ...) at most 2 rows name the same one
- tile_row: int32 [16384], P(('grp', 'inner')), may hold values from 0 to 3
- tile_col: int32 [16384], P(('grp', 'inner')), may hold values from 0 to 127
Outputs:
- ladder: float32 [1024, 16384], P(('grp', 'inner'))
Inputs may be any that keep to these rules, and one draw needn't show every extreme that they name: `tile_owner`: among the 128 tiles of one device no owner is named more than 2 times, a bound that some block reaches.
All inputs are finite; a program needn't handle non-finite values.
Results may differ from a plain program's by a relative error of at most 0.0001.
Values sent between devices are 32-bit elements; how exact they have to be, the bound alone decides.
No kernel may reach another device: no remote copies, remote signals or barrier semaphores. Data moves between devices by JAX's collectives and lax.ppermute only.
A program may use at most 192 MiB of HBM per device.

v0:
```python
import jax
import jax.numpy as jnp
from jax import lax
from jax.sharding import PartitionSpec as P


def per_device(amplitude, integrals, tile_owner, tile_row, tile_col):
    n_grp = lax.axis_size("grp")
    n_inner = lax.axis_size("inner")
    devices = n_grp * n_inner
    rows_dev, width_all = amplitude.shape
    tile_count, tile_size = (integrals.shape[0], integrals.shape[1])
    blocks = width_all // tile_size
    per_dev = blocks // n_inner
    capacity = max(2, 2 * tile_count // devices)
    owners = tile_owner[:, 0]
    onehot = (owners[:, None] == jnp.arange(devices, dtype=jnp.int32)[None, :]).astype(jnp.int32)
    rank_within = jnp.sum((jnp.cumsum(onehot, axis=0) - onehot) * onehot, axis=1)
    slot_index = owners * capacity + rank_within
    position = (tile_row * blocks + tile_col).astype(jnp.float32)
    send_tiles = (
        jnp.zeros((devices * capacity, tile_size, tile_size), jnp.float32)
        .at[slot_index]
        .set(integrals)
    )
    send_place = jnp.zeros((devices * capacity,), jnp.float32).at[slot_index].set(position)
    got_tiles, got_place = (
        lax.all_to_all(send_tiles, ("grp", "inner"), split_axis=0, concat_axis=0, tiled=True),
        lax.all_to_all(send_place, ("grp", "inner"), split_axis=0, concat_axis=0, tiled=True),
    )
    place_index = got_place.astype(jnp.int32)
    assembled = (
        jnp.zeros((per_dev * blocks, tile_size, tile_size), jnp.float32)
        .at[place_index]
        .add(got_tiles)
    )
    dense_blocks = (
        assembled.reshape(per_dev, blocks, tile_size, tile_size)
        .transpose(0, 2, 1, 3)
        .reshape(per_dev * tile_size, blocks * tile_size)
    )
    slab_amplitude = lax.all_to_all(amplitude, "inner", split_axis=1, concat_axis=0, tiled=True)
    return lax.psum_scatter(
        jnp.dot(
            slab_amplitude,
            dense_blocks,
            precision=lax.Precision.HIGHEST,
            preferred_element_type=jnp.float32,
        ),
        "inner",
        scatter_dimension=0,
        tiled=True,
    )


def solution(mesh):
    placed = (
        P(("grp", "inner"), None),
        P(("grp", "inner"), None, None),
        P(("grp", "inner"), None),
        P(("grp", "inner")),
        P(("grp", "inner")),
    )
    return jax.shard_map(
        per_device, mesh=mesh, in_specs=placed, out_specs=P(("grp", "inner"), None), check_vma=False
    )
```

profile of v0, /device:TPU:0, one launch (start us, length us, event | category | flops | bytes accessed | tf_op | source)
XLA Modules:
  0.0 571.1 jit_solution(5504528757039858345)
XLA Ops:
  6.5 0.7 fusion.7
  7.3 0.2 reduce_window_sum.11
  7.4 0.8 select_reduce_fusion
  8.3 0.7 fusion.8
  8.9 0.7 add_convert_fusion
  9.6 1.0 scatter_custom_fusion
  10.6 0.8 all_to_all.23
  11.4 11.1 %all-to-all-start = ((f32[128,2,1]{1,2,0:T(1,128)}), f32[128,2,1]{1,2,0:T(1,128)S(1)}, u32[]{:S(2)}, u32[]{:S(2)}) async-start(f32[128,2,1]{1,2,0:T(1,128)} %bitcast.3), calls=%async_computation | async-start | bytes 131072 | tf_op jit(solution)/shard_map/all_to_all | solution.py:29
  22.5 7.8 %broadcast_in_dim.15 = f32[256,128,128]{2,1,0:T(8,128)} broadcast(f32[]{:T(128)} %constant.6.clone.1), dimensions={} | broadcast | bytes 16777220 | tf_op jit(solution)/shard_map/broadcast_in_dim | solution.py:22
  30.4 23.4 %scatter_fusion = f32[256,128,128]{2,1,0:T(8,128)} fusion(f32[256,128,128]{2,1,0:T(8,128)} %broadcast_in_dim.15, s32[128]{0:T(128)S(1)} %fusion.8, f32[128,128,128]{2,1,0:T(8,128)} %param.6), kind=kCustom, calls=%fused_computation.1 | custom fusion | bytes 25166336 | tf_op jit(solution)/shard_map/scatter | solution.py:24
  53.7 0.0 all-to-all-done
  53.7 197.7 %all_to_all.33 = f32[256,128,128]{2,1,0:T(8,128)} all-to-all(f32[256,128,128]{2,1,0:T(8,128)} %scatter_fusion), channel_id=1, replica_groups=mesh['grp'=4,'inner'=32] {'grp','inner'}, dimensions={0} | all-to-all | bytes 33554432 | tf_op jit(solution)/shard_map/all_to_all | solution.py:28
  251.4 6.9 %all-to-all-start.2 = ((f32[8,32,512]{2,0,1:T(8,128)}), f32[8,32,512]{2,0,1:T(8,128)S(1)}, u32[]{:S(2)}, u32[]{:S(2)}) async-start(f32[8,32,512]{2,0,1:T(8,128)} %bitcast.7), calls=%async_computation.2 | async-start | bytes 1048576 | tf_op jit(solution)/shard_map/all_to_all | solution.py:42
  258.3 0.0 reduce-scatter.4.cloned.1.call-start
  258.4 0.2 convert_reduce_fusion
  258.6 0.1 convert_element_type.22
  258.7 11.2 %broadcast_in_dim.6 = f32[512,128,128]{2,1,0:T(8,128)} broadcast(f32[]{:T(128)} %constant.6.clone.1), dimensions={} | broadcast | bytes 33554436 | tf_op jit(solution)/shard_map/broadcast_in_dim | solution.py:33
  270.0 50.2 %scatter_fusion.1 = f32[512,128,128]{2,1,0:T(8,128)} fusion(f32[512,128,128]{2,1,0:T(8,128)} %broadcast_in_dim.6, s32[256]{0:T(256)S(1)} %bitcast.30, f32[256,128,128]{2,1,0:T(8,128)} %all_to_all.33), kind=kCustom, calls=%fused_computation.2 | custom fusion | flops 4194304 | bytes 50332672 | tf_op jit(solution)/shard_map/scatter-add | solution.py:35
  320.2 31.8 %copy.11 = f32[4,128,128,128]{3,2,1,0:T(8,128)} copy(f32[4,128,128,128]{3,1,2,0:T(8,128)} %bitcast.28) | data formatting | bytes 67108864 | tf_op jit(solution)/shard_map/transpose | solution.py:39
  352.0 0.0 all-to-all-done.2
  352.0 76.3 %fusion.3 = f32[256,16384]{0,1:T(8,128)} fusion(f32[64,8,128,128]{3,2,1,0:T(8,128)} %bitcast.29, f32[8,32,512]{2,0,1:T(8,128)S(1)} %all-to-all-done.2), kind=kOutput, calls=%fused_computation.6 | convolution fusion | flops 25769803776 | bytes 50855936 | tf_op jit(solution)/shard_map/dot_general | solution.py:44
  428.3 17.4 %copy.13 = f32[256,16384]{1,0:T(8,128)} copy(f32[256,16384]{0,1:T(8,128)} %fusion.3) | data formatting | bytes 33554432
  445.7 0.0 reduce-scatter.4.cloned.1.call-update
  445.8 118.5 %reduce-scatter.4.cloned.1.call-done = f32[8,16384]{1,0:T(8,128)} async-done(((f32[256,16384]{1,0:T(8,128)}), f32[8,16384]{1,0:T(8,128)}) %reduce-scatter.4.cloned.1.call-update) | async-done | bytes 524304 | tf_op jit(solution)/shard_map/reduce_scatter | solution.py:43
  (1 shorter events, 0.0 us)
Async XLA Ops:
  11.4 42.4 %all-to-all-start = ((f32[128,2,1]{1,2,0:T(1,128)}), f32[128,2,1]{1,2,0:T(1,128)S(1)}, u32[]{:S(2)}, u32[]{:S(2)}) async-start(f32[128,2,1]{1,2,0:T(1,128)} %bitcast.3), calls=%async_computation | async-start | bytes 131072 | tf_op jit(solution)/shard_map/all_to_all | solution.py:29
  251.4 100.6 %all-to-all-start.2 = ((f32[8,32,512]{2,0,1:T(8,128)}), f32[8,32,512]{2,0,1:T(8,128)S(1)}, u32[]{:S(2)}, u32[]{:S(2)}) async-start(f32[8,32,512]{2,0,1:T(8,128)} %bitcast.7), calls=%async_computation.2 | async-start | bytes 1048576 | tf_op jit(solution)/shard_map/all_to_all | solution.py:42
  258.3 305.9 %reduce-scatter.4.cloned.1.call-start = ((), (), s32[]{:S(2)}) async-start(), calls=%async_computation.4 | async-start | bytes 17301504 | tf_op jit(solution)/shard_map/reduce_scatter | solution.py:43
Sparse Core Ops, SparseCore 0:
  445.9 118.3 reduce-scatter.3
where the time goes:
time: 573 us; the launch traced here: 571 us
  blocking collectives  198 us (35%)
  waiting for transfers between devices  119 us (21%)
  local copies, waits for them, and re-layouts  93.6 us (16%)
  matrix products  76.3 us (13%)
  other arithmetic  53.5 us (9%)
  starting transfers between devices  18.1 us (3%)
  between operations  13.5 us (2%)
    all_to_all x1, blocking collectives, per_device(): lax.all_to_all(send_tiles, ('grp', 'inner'), split_axis=0, concat_axis=0,...  198 us
    reduce_scatter x1, waiting for transfers between devices, per_device(): lax.psum_scatter(jnp.dot(slab_amplitude, dense_blocks, precision=lax.Prec...  118 us
    dot_general x1, matrix products, per_device(): jnp.dot(slab_amplitude, dense_blocks, precision=lax.Precision.HIGHEST, pr...  76.3 us
    scatter-add x1, other arithmetic, per_device(): assembled = jnp.zeros((per_dev * blocks, tile_size, tile_size), jnp.float...  50.2 us
    transpose x1, local copies, waits for them, and re-layouts, per_device(): dense_blocks = assembled.reshape(per_dev, blocks, tile_size, tile_size).t...  31.8 us
    scatter x1, local copies, waits for them, and re-layouts, per_device(): send_tiles = jnp.zeros((devices * capacity, tile_size, tile_size), jnp.fl...  23.4 us
    unnamed x1, local copies, waits for them, and re-layouts  17.4 us
  transfers between devices with their start and end apart: 3, of which 1 were waited for; matrix products, arithmetic and copies ran while one was open for 22% of the time, Pallas kernels for 0%

commit v1 on v0

v1 whole, which is shorter than its diff:
```python
import functools

import jax
import jax.numpy as jnp
from jax import lax
from jax.experimental import pallas as pl
from jax.experimental.pallas import tpu as pltpu
from jax.sharding import PartitionSpec as P

TILE = 128
STARTS = (0, 14, 27, 40)
OPEN = (0, 0, 0, 128)
VMEM = 50 * 1024 * 1024
AXES = ("grp", "inner")


def slow_part(amplitude, integrals, tile_owner, tile_row, tile_col):
    n_grp, n_inner = lax.axis_size("grp"), lax.axis_size("inner")
    devices = n_grp * n_inner
    count, size = integrals.shape[:2]
    blocks = amplitude.shape[1] // size
    per_dev = blocks // n_inner
    capacity = max(2, 2 * count // devices)
    owners = tile_owner[:, 0]
    order = jnp.arange(count, dtype=jnp.int32)
    same = (owners[:, None] == owners[None, :]) & (order[None, :] < order[:, None])
    slot = owners * capacity + jnp.sum(same.astype(jnp.int32), axis=1)
    position = (tile_row * blocks + tile_col).astype(jnp.float32)
    tiles = jnp.zeros((devices * capacity, size, size), jnp.float32).at[slot].set(integrals)
    place = jnp.zeros((devices * capacity,), jnp.float32).at[slot].set(position)
    tiles, place = (
        lax.all_to_all(tiles, AXES, split_axis=0, concat_axis=0, tiled=True),
        lax.all_to_all(place, AXES, split_axis=0, concat_axis=0, tiled=True),
    )
    dense = jnp.zeros((per_dev * blocks, size, size), jnp.float32).at[place.astype(jnp.int32)].add(tiles)
    dense = dense.reshape(per_dev, blocks, size, size).transpose(0, 2, 1, 3).reshape(per_dev * size, blocks * size)
    slab = lax.all_to_all(amplitude, "inner", split_axis=1, concat_axis=0, tiled=True)
    return lax.psum_scatter(
        jnp.dot(slab, dense, precision=lax.Precision.HIGHEST, preferred_element_type=jnp.float32),
        "inner",
        scatter_dimension=0,
        tiled=True,
    )


def pack_kernel(count, lists, first, index, tiles, *refs):
    outs, sems = refs[-len(lists) - 1 : -1], refs[-1]
    for at, which in enumerate(lists):

        def issue(k, _):
            pltpu.make_async_copy(tiles.at[index[which * first[1] + first[0] + k]], outs[at].at[k], sems.at[at]).start()
            return 0

        lax.fori_loop(0, count, issue, 0)
    for at in range(len(lists)):
        pltpu.make_async_copy(tiles.at[pl.ds(0, count)], outs[at], sems.at[at]).wait()


def pack(integrals, index, lists, start, count, total, after):
    any_spec = pl.BlockSpec(memory_space=pl.ANY)
    return pl.pallas_call(
        functools.partial(pack_kernel, count, lists, (start, total)),
        out_shape=[jax.ShapeDtypeStruct((count, TILE, TILE), jnp.float32)] * len(lists),
        in_specs=[pl.BlockSpec(memory_space=pltpu.SMEM), any_spec] + [any_spec] * len(after),
        out_specs=[any_spec] * len(lists),
        scratch_shapes=[pltpu.SemaphoreType.DMA((len(lists),))],
        cost_estimate=pl.CostEstimate(flops=0, bytes_accessed=2 * len(lists) * count * TILE * TILE * 4, transcendentals=0),
    )(index, integrals, *after)


def split(value):
    high = value.astype(jnp.bfloat16)
    return high, (value - high.astype(jnp.float32)).astype(jnp.bfloat16)


def ladder_kernel(count, lists, low, open_col, blocks, has_acc, *refs):
    refs = list(refs)
    code, where, amp = refs[:3]
    del refs[:3]
    acc_in = refs.pop(0) if has_acc else None
    tiles = refs[:lists]
    del refs[:lists]
    acc_out = refs.pop(0) if open_col < blocks else None
    parts = [refs.pop(0) for _ in range(8)] if open_col > low else []
    amp_v, acc_v, tile_v, amp_sem, acc_sem, tile_sem, out_sem = refs

    z, x = where[0], where[1]
    for sx in range(4):
        for sz in range(4):
            source = lax.rem(z + sz, 4) * 4 + lax.rem(x + sx, 4)
            pltpu.make_async_copy(amp.at[source], amp_v.at[sx * 4 + sz], amp_sem).start()
    if has_acc:
        acc_copy = pltpu.make_async_copy(acc_in, acc_v, acc_sem)
        acc_copy.start()
    copies = [pltpu.make_async_copy(tiles[k], tile_v.at[k], tile_sem.at[k]) for k in range(lists)]
    for copy in copies:
        copy.start()
    if has_acc:
        acc_copy.wait()
    else:
        acc_v[...] = jnp.zeros_like(acc_v)
    pltpu.make_async_copy(amp, amp_v, amp_sem).wait()

    for k in range(lists):
        copies[k].wait()

        def one(j, _):
            place = code[k * count + j]

            @pl.when(place >= 0)
            def _():
                row = pl.multiple_of((place // blocks) * TILE, TILE)
                col = pl.multiple_of((lax.rem(place, blocks) - low) * TILE, TILE)
                a_hi, a_lo = split(amp_v[:, :, pl.ds(row, TILE)].reshape(16 * 8, TILE))
                t_hi, t_lo = split(tile_v[k, j])
                left = jnp.concatenate([a_hi, a_lo], axis=1)
                right = jnp.concatenate([t_hi, t_lo], axis=1)
                both = jnp.dot(left, jnp.concatenate([right, right], axis=0), preferred_element_type=jnp.float32)
                term = both[:, :TILE] + both[:, TILE:]
                acc_v[:, :, :, pl.ds(col, TILE)] += term.reshape(4, 4, 8, TILE)

            return 0

        lax.fori_loop(0, count, one, 0)

    done = []
    if acc_out is not None:
        done.append(pltpu.make_async_copy(acc_v.at[:, :, :, pl.ds((open_col - low) * TILE, (blocks - open_col) * TILE)], acc_out, out_sem.at[8]))
    if parts:
        half = (open_col - low) * TILE // 2
        for s in range(4):
            done.append(pltpu.make_async_copy(acc_v.at[s, :, :, pl.ds(0, half)], parts[s], out_sem.at[s]))
            done.append(pltpu.make_async_copy(acc_v.at[:, s, :, pl.ds(half, half)], parts[4 + s], out_sem.at[4 + s]))
    for copy in done:
        copy.start()
    for copy in done:
        copy.wait()


def ladder(code, where, amp, acc, tiles, low, open_col, blocks):
    lists, count = len(tiles), tiles[0].shape[0]
    any_spec, smem = pl.BlockSpec(memory_space=pl.ANY), pl.BlockSpec(memory_space=pltpu.SMEM)
    shapes = []
    if open_col < blocks:
        shapes.append(jax.ShapeDtypeStruct((4, 4, 8, (blocks - open_col) * TILE), jnp.float32))
    if open_col > low:
        shapes += [jax.ShapeDtypeStruct((4, 8, (open_col - low) * TILE // 2), jnp.float32)] * 8
    given = [code, where, amp] + ([] if acc is None else [acc]) + list(tiles)
    outs = pl.pallas_call(
        functools.partial(ladder_kernel, count, lists, low, open_col, blocks, acc is not None),
        out_shape=shapes,
        in_specs=[smem, smem] + [any_spec] * (len(given) - 2),
        out_specs=[any_spec] * len(shapes),
        scratch_shapes=[
            pltpu.VMEM((16, 8, blocks * TILE), jnp.float32),
            pltpu.VMEM((4, 4, 8, (blocks - low) * TILE), jnp.float32),
            pltpu.VMEM((lists, count, TILE, TILE), jnp.float32),
            pltpu.SemaphoreType.DMA,
            pltpu.SemaphoreType.DMA,
            pltpu.SemaphoreType.DMA((lists,)),
            pltpu.SemaphoreType.DMA((9,)),
        ],
        compiler_params=pltpu.CompilerParams(vmem_limit_bytes=VMEM),
        cost_estimate=pl.CostEstimate(flops=lists * count * 2 * 128**3 * 4, bytes_accessed=24 * 2**20, transcendentals=0),
    )(*given)
    outs = list(outs)
    acc = outs.pop(0) if open_col < blocks else None
    return acc, outs


def per_device(amplitude, integrals, tile_owner, tile_row, tile_col):
    n_grp, n_inner = lax.axis_size("grp"), lax.axis_size("inner")
    devices = n_grp * n_inner
    rows, width = amplitude.shape
    count = integrals.shape[0]
    blocks = width // TILE
    per_dev = blocks // n_inner
    total = STARTS[-1]
    chunks = len(STARTS) - 1
    grp, inner = lax.axis_index("grp"), lax.axis_index("inner")
    z, x, core = inner // 8, (inner // 2) % 4, inner % 2

    def at(z, x, core):
        return (z % 4) * 8 + (x % 4) * 2 + core

    every = [(a, b, c) for a in range(4) for b in range(4) for c in range(2)]
    along_x = {s: [(at(a, b, c), at(a, b + s, c)) for a, b, c in every] for s in (1, 2, 3)}
    along_z = {s: [(at(a, b, c), at(a + s, b, c)) for a, b, c in every] for s in (1, 2, 3)}
    along_y = {s: [(i, (i + s) % n_grp) for i in range(n_grp)] for s in (1, 2, 3)}
    across = [(i, i ^ 1) for i in range(n_inner)]
    same_core = [[at(a, b, c) for a in range(4) for b in range(4)] for c in range(2)]

    amp = lax.all_gather(amplitude, "inner", axis=0, axis_index_groups=same_core)

    owners = tile_owner[:, 0]
    slab = owners // n_inner
    step = (slab - grp + n_grp) % n_grp
    order = jnp.arange(count, dtype=jnp.int32)
    key = tile_col * count + order
    ahead = (slab[:, None] == slab[None, :]) & (key[None, :] < key[:, None])
    rank = jnp.sum(ahead.astype(jnp.int32), axis=1)
    limit = jnp.full((count,), total, jnp.int32)
    for c in range(chunks - 1, 0, -1):
        limit = jnp.where(tile_col < OPEN[c], STARTS[c], limit)
    fits = rank < limit
    code = ((owners % n_inner) * per_dev + tile_row) * blocks + tile_col
    slots = jnp.arange(n_grp * total, dtype=jnp.int32)[:, None]
    mine = jnp.where(fits, step * total + rank, -1)[None, :] == slots
    index = jnp.sum(jnp.where(mine, order[None, :], 0), axis=1)
    theirs = jnp.where(fits, slab * total + rank, -1)[None, :] == slots
    codes = jnp.sum(jnp.where(theirs, code[None, :] + 1, 0), axis=1) - 1
    left_over = jnp.sum((~fits).astype(jnp.int32))

    got = []
    before_a, before_b = (), ()
    for c in range(chunks):
        lo, n = STARTS[c], STARTS[c + 1] - STARTS[c]
        p1, p3 = pack(integrals, index, (1, 3), lo, n, total, before_a)
        p2, p0 = pack(integrals, index, (2, 0), lo, n, total, before_b)
        r1, r3 = lax.ppermute(p1, "grp", along_y[1]), lax.ppermute(p3, "grp", along_y[3])
        r2 = lax.ppermute(p2, "grp", along_y[2])
        before_a, before_b = (r1, r3), (r2,)
        got.append((p0, r1, r2, r3))
        if c == 0:
            gate = p2
    codes, _ = lax.optimization_barrier((codes, gate))
    note = jnp.concatenate(
        [
            jnp.broadcast_to(codes.reshape(n_grp, 1, total), (n_grp, n_inner, total)),
            jnp.broadcast_to(left_over, (n_grp, n_inner, 1)),
        ],
        axis=2,
    ).astype(jnp.float32)
    note = lax.all_to_all(note.reshape(devices, total + 1), AXES, split_axis=0, concat_axis=0, tiled=True)
    overflow = jnp.sum(note[:, total]) > 0.5
    note = note[:, :total].reshape(n_grp, n_inner // 2, 2, total)
    note = lax.dynamic_index_in_dim(note, inner // 2, axis=1, keepdims=False)
    note = jnp.stack([lax.dynamic_index_in_dim(note, (grp - s + n_grp) % n_grp, axis=0, keepdims=False) for s in range(4)])
    note = jnp.stack([lax.dynamic_index_in_dim(note, core, axis=1, keepdims=False), lax.dynamic_index_in_dim(note, 1 - core, axis=1, keepdims=False)])
    note = note.astype(jnp.int32)
    where = jnp.stack([z, x]).astype(jnp.int32)

    acc, pieces = None, []
    for c in range(chunks):
        own = got[c]
        other = [lax.ppermute(t, "inner", across) for t in own]
        code_c = note[:, :, STARTS[c] : STARTS[c + 1]].reshape(-1)
        acc, parts = ladder(code_c, where, amp, acc, [*own, *other], OPEN[c], OPEN[c + 1], blocks)
        if parts:
            one, two = parts[:4], parts[4:]
            r1 = [lax.ppermute(one[s], "inner", along_x[s]) for s in (1, 3, 2)]
            r2 = [lax.ppermute(two[s], "inner", along_z[s]) for s in (1, 3, 2)]
            s1 = [one[0][q] + r1[0][q] + r1[1][q] + r1[2][q] for q in range(4)]
            s2 = [two[0][q] + r2[0][q] + r2[1][q] + r2[2][q] for q in range(4)]
            f1 = [lax.ppermute(s1[s], "inner", along_z[s]) for s in (1, 3, 2)]
            f2 = [lax.ppermute(s2[s], "inner", along_x[s]) for s in (1, 3, 2)]
            pieces += [s1[0] + f1[0] + f1[1] + f1[2], s2[0] + f2[0] + f2[1] + f2[2]]
    out = jnp.concatenate(pieces, axis=1)

    def with_rest(out):
        rest = jnp.where(fits[:, None, None], 0.0, integrals)
        return out + slow_part(amplitude, rest, tile_owner, tile_row, tile_col)

    return lax.cond(overflow, with_rest, lambda out: out, out)


def solution(mesh):
    placed = (P(AXES, None), P(AXES, None, None), P(AXES, None), P(AXES), P(AXES))
    return jax.shard_map(per_device, mesh=mesh, in_specs=placed, out_specs=P(AXES, None), check_vma=False)
```

time: 573 us -> 607 us (1.059); the launches traced: 571 us -> 597 us
  Pallas kernels: 0 us -> 400 us
  blocking collectives: 198 us -> 0 us
  local copies, waits for them, and re-layouts: 93.6 us -> 15.6 us
  matrix products: 76.3 us -> 0 us
  starting transfers between devices: 18.1 us -> 65.1 us
  other arithmetic: 53.5 us -> 11.2 us
  waiting for transfers between devices: 119 us -> 90.2 us
    pallas_call x0 -> x9, Pallas kernels: none -> 400 us  [the longest x6 328 us: pack(): pl.pallas_call(functools.partial(pack_kernel, count, lists, (start, total...]
    all_to_all x1 -> x0, blocking collectives: 198 us -> none  [per_device(): lax.all_to_all(send_tiles, ('grp', 'inner'), split_axis=0, concat_axis=0,...]
    reduce_scatter x1 -> x0, waiting for transfers between devices: 118 us -> none  [per_device(): lax.psum_scatter(jnp.dot(slab_amplitude, dense_blocks, precision=lax.Prec...]
    dot_general x1 -> x0, matrix products: 76.3 us -> none  [per_device(): jnp.dot(slab_amplitude, dense_blocks, precision=lax.Precision.HIGHEST, pr...]
    ppermute x0 -> x33, waiting for transfers between devices: none -> 61.2 us  [the longest x3 21.3 us: per_device(): r2 = lax.ppermute(p2, 'grp', along_y[2])]
    ppermute x0 -> x33, starting transfers between devices: none -> 53.7 us  [the longest x3 27.7 us: per_device(): r2 = [lax.ppermute(two[s], 'inner', along_z[s]) for s in (1, 3, 2)]]
    scatter-add x1 -> x0, other arithmetic: 50.2 us -> none  [per_device(): assembled = jnp.zeros((per_dev * blocks, tile_size, tile_size), jnp.float...]
    transpose x1 -> x0, local copies, waits for them, and re-layouts: 31.8 us -> none  [per_device(): dense_blocks = assembled.reshape(per_dev, blocks, tile_size, tile_size).t...]
  transfers between devices with their start and end apart: 3 -> 35, of which waited for: 1 -> 6; matrix products, arithmetic and copies ran while one was open for 22% -> 2% of each run, Pallas kernels for 0% -> 64%
where the time goes in v1:
time: 607 us; the launch traced here: 597 us
  Pallas kernels  400 us (66%)
  waiting for transfers between devices  90.2 us (15%)
  starting transfers between devices  65.1 us (11%)
  local copies, waits for them, and re-layouts  15.6 us (3%)
  between operations  14.5 us (2%)
  other arithmetic  11.2 us (2%)
    pallas_call x6, Pallas kernels, pack(): pl.pallas_call(functools.partial(pack_kernel, count, lists, (start, total...  328 us
    pallas_call x3, Pallas kernels, ladder(): pl.pallas_call(functools.partial(ladder_kernel, count, lists, low, open_c...  71.9 us
    all_to_all x1, waiting for transfers between devices, per_device(): lax.all_to_all(note.reshape(devices, total + 1), AXES, split_axis=0, conc...  28.3 us
    ppermute x3, starting transfers between devices, per_device(): r2 = [lax.ppermute(two[s], 'inner', along_z[s]) for s in (1, 3, 2)]  27.7 us
    ppermute x3, waiting for transfers between devices, per_device(): r2 = lax.ppermute(p2, 'grp', along_y[2])  21.3 us
    ppermute x3, waiting for transfers between devices, per_device(): r1 = [lax.ppermute(one[s], 'inner', along_x[s]) for s in (1, 3, 2)]  17.4 us
    ppermute x3, waiting for transfers between devices, per_device(): r2 = [lax.ppermute(two[s], 'inner', along_z[s]) for s in (1, 3, 2)]  13.7 us
  transfers between devices with their start and end apart: 35, of which 6 were waited for; matrix products, arithmetic and copies ran while one was open for 2% of the time, Pallas kernels for 64%

profile of v1, /device:TPU:0, one launch (start us, length us, event | category | flops | bytes accessed | tf_op | source)
XLA Modules:
  0.0 597.0 jit_solution(2562091097462831387)
XLA Ops:
  6.5 0.7 all-gather.3.cloned.1.call-update
  7.3 0.7 fusion.37
  7.9 0.7 and_select_fusion.2
  8.6 0.2 convert_reduce_fusion.2
  8.8 1.4 fusion.35
  10.2 0.7 select_reduce_fusion.index
  10.9 57.4 %shard_map.58 = (f32[14,128,128]{2,1,0:T(8,128)}, f32[14,128,128]{2,1,0:T(8,128)}) custom-call(s32[160]{0:T(256)} %select_reduce_fusion.index, f32[128,128,128]{2,1,0:T(8,128)} %tiles.11), custom_call_target="tpu_custom_call" | custom-call | bytes 3670016 | tf_op jit(solution)/shard_map/pallas_call | solution.py:61
  68.3 1.7 collective-permute-start
  70.0 1.6 collective-permute-start.2
  71.6 57.4 %shard_map.57 = (f32[14,128,128]{2,1,0:T(8,128)}, f32[14,128,128]{2,1,0:T(8,128)}) custom-call(s32[160]{0:T(256)} %select_reduce_fusion.index, f32[128,128,128]{2,1,0:T(8,128)} %tiles.11), custom_call_target="tpu_custom_call" | custom-call | bytes 3670016 | tf_op jit(solution)/shard_map/pallas_call | solution.py:61
  129.0 2.1 collective-permute-start.1
  131.2 0.9 copy-done.2
  132.1 0.9 copy-done.4
  133.1 53.4 %shard_map.61 = (f32[13,128,128]{2,1,0:T(8,128)}, f32[13,128,128]{2,1,0:T(8,128)}) custom-call(s32[160]{0:T(256)} %select_reduce_fusion.index, f32[128,128,128]{2,1,0:T(8,128)} %tiles.11, f32[14,128,128]{2,1,0:T(8,128)} %copy-done.2, f32[14,128,128]{2,1,0:T(8,128)} %copy-done.4), custom_call_target="tpu_custom_call" | custom-call | bytes 3407872 | tf_op jit(solution)/shard_map/pallas_call | solution.py:61
  186.5 0.7 collective-permute-start.7
  187.3 2.6 collective-permute-start.9
  189.8 1.0 copy-done
  190.8 53.4 %shard_map.60 = (f32[13,128,128]{2,1,0:T(8,128)}, f32[13,128,128]{2,1,0:T(8,128)}) custom-call(s32[160]{0:T(256)} %select_reduce_fusion.index, f32[128,128,128]{2,1,0:T(8,128)} %tiles.11, f32[14,128,128]{2,1,0:T(8,128)} %copy-done), custom_call_target="tpu_custom_call" | custom-call | bytes 3407872 | tf_op jit(solution)/shard_map/pallas_call | solution.py:61
  244.2 0.3 collective-permute-start.8
  244.6 0.5 collective-permute-start.4
  245.1 0.1 collective-permute-start.6
  245.2 0.4 collective-permute-start.10
  245.6 21.3 %collective-permute-done.8.refs_6_.refs_0_ = f32[13,128,128]{2,1,0:T(8,128)} collective-permute-done((f32[13,128,128]{2,1,0:T(8,128)}, f32[13,128,128]{2,1,0:T(8,128)}, u32[]{:S(2)}, u32[]{:S(2)}) %collective-permute-start.8) | collective-permute-done | bytes 852000 | tf_op jit(solution)/shard_map/ppermute | solution.py:221
  266.9 53.4 %shard_map.64 = (f32[13,128,128]{2,1,0:T(8,128)}, f32[13,128,128]{2,1,0:T(8,128)}) custom-call(s32[160]{0:T(256)} %select_reduce_fusion.index, f32[128,128,128]{2,1,0:T(8,128)} %tiles.11, f32[13,128,128]{2,1,0:T(8,128)} %collective-permute-done.7.refs_5_.refs_0_, f32[13,128,128]{2,1,0:T(8,128)} %collective-permute-done.9.refs_7_.refs_1_), custom_call_target="tpu_custom_call" | custom-call | bytes 3407872 | tf_op jit(solution)/shard_map/pallas_call | solution.py:61
  320.4 53.4 %shard_map.63 = (f32[13,128,128]{2,1,0:T(8,128)}, f32[13,128,128]{2,1,0:T(8,128)}) custom-call(s32[160]{0:T(256)} %select_reduce_fusion.index, f32[128,128,128]{2,1,0:T(8,128)} %tiles.11, f32[13,128,128]{2,1,0:T(8,128)} %collective-permute-done.8.refs_6_.refs_0_), custom_call_target="tpu_custom_call" | custom-call | bytes 3407872 | tf_op jit(solution)/shard_map/pallas_call | solution.py:61
  373.8 0.6 collective-permute-start.13
  374.4 3.2 collective-permute-start.16
  377.7 0.1 select_reduce_fusion.1
  377.8 0.1 broadcast_in_dim.68
  377.9 1.3 pad_convert_fusion
  379.2 11.4 %all-to-all-start.3 = ((f32[128,1,41]{2,1,0:T(1,128)}), f32[128,1,41]{2,1,0:T(1,128)S(1)}, u32[]{:S(2)}, u32[]{:S(2)}) async-start(f32[128,1,41]{2,1,0:T(1,128)} %bitcast.13), calls=%async_computation.4 | async-start | bytes 131072 | tf_op jit(solution)/shard_map/all_to_all | solution.py:234
  390.9 28.3 %all-to-all-done.3 = f32[128,1,41]{2,1,0:T(1,128)S(1)} async-done(((f32[128,1,41]{2,1,0:T(1,128)}), f32[128,1,41]{2,1,0:T(1,128)S(1)}, u32[]{:S(2)}, u32[]{:S(2)}) %all-to-all-start.3) | async-done | bytes 21024 | tf_op jit(solution)/shard_map/all_to_all | solution.py:234
  419.2 0.1 collective-permute-start.17
  419.3 0.5 collective-permute-start.18
  419.8 0.1 collective-permute-start.20
  419.9 0.4 collective-permute-start.19
  420.3 0.1 reshape.119.refs_0_
  420.5 0.1 reshape.118.refs_0_
  420.6 0.1 reshape.117.refs_0_
  420.7 1.2 copy-done.6
  421.9 26.7 %shard_map.59.refs_3_ = f32[4,4,8,16384]{3,2,1,0:T(8,128)} custom-call(s32[112]{0:T(128)S(1)} %reshape.119.refs_0_, s32[2]{0:T(128)S(1)} %pad_add_fusion.refs_1_, f32[16,8,16384]{2,1,0:T(8,128)} %bitcast.93, f32[14,128,128]{2,1,0:T(8,128)S(1)} %copy-done.6, f32[14,128,128]{2,1,0:T(8,128)S(1)} %copy-done.3, f32[14,128,128]{2,1,0:T(8,128)S(1)} %copy-done.1, ...), custom_call_target="tpu_custom_call" | custom-call | flops 1879048192 | bytes 25165824 | tf_op jit(solution)/shard_map/pallas_call | solution.py:149
  448.6 27.9 %shard_map.62.refs_3_ = f32[4,4,8,16384]{3,2,1,0:T(8,128)} custom-call(s32[104]{0:T(128)S(1)} %reshape.118.refs_0_, s32[2]{0:T(128)S(1)} %pad_add_fusion.refs_1_, f32[16,8,16384]{2,1,0:T(8,128)} %bitcast.94, f32[4,4,8,16384]{3,2,1,0:T(8,128)} %shard_map.59.refs_3_, f32[13,128,128]{2,1,0:T(8,128)S(1)} %copy-done.7, ...), custom_call_target="tpu_custom_call" | custom-call | flops 1744830464 | bytes 25165824 | tf_op jit(solution)/shard_map/pallas_call | solution.py:149
  476.6 17.3 %shard_map.65 = (f32[4,8,8192]{2,1,0:T(8,128)}, f32[4,8,8192]{2,1,0:T(8,128)}, f32[4,8,8192]{2,1,0:T(8,128)}, f32[4,8,8192]{2,1,0:T(8,128)}, f32[4,8,8192]{2,1,0...) custom-call(s32[104]{0:T(128)S(1)} %reshape.117.refs_0_, ...), custom_call_target="tpu_custom_call" | custom-call | flops 1744830464 | bytes 25165824 | tf_op jit(solution)/shard_map/pallas_call | solution.py:149
  493.9 1.2 collective-permute-start.21
  495.1 2.1 collective-permute-start.22
  497.2 1.0 collective-permute-start.23
  498.2 0.7 slice_reduce_fusion
  499.5 2.2 collective-permute-start.27
  501.7 1.4 collective-permute-start.28
  503.1 17.4 %collective-permute-done.21 = f32[4,8,8192]{2,1,0:T(8,128)S(1)} collective-permute-done((f32[4,8,8192]{2,1,0:T(8,128)}, f32[4,8,8192]{2,1,0:T(8,128)S(1)}, u32[]{:S(2)}, u32[]{:S(2)}) %collective-permute-start.21) | collective-permute-done | bytes 1048608 | tf_op jit(solution)/shard_map/ppermute | solution.py:251
  520.6 24.1 %collective-permute-start.29 = (f32[4,8,8192]{2,1,0:T(8,128)}, f32[4,8,8192]{2,1,0:T(8,128)S(1)}, u32[]{:S(2)}, u32[]{:S(2)}) collective-permute-start(f32[4,8,8192]{2,1,0:T(8,128)} %get-tuple-element.71), channel_id=1, source_target_pairs={{0,16},{1,17},{2,18},{3,19},{4,20},{5,21},{6,22},{7,23},{8,24},{9,... | collective-permute-start | bytes 3145736 | tf_op jit(solution)/shard_map/ppermute | solution.py:252
  544.7 1.7 fusion.20
  546.4 0.2 collective-permute-start.24
  546.6 3.1 collective-permute-start.25
  549.7 13.7 %collective-permute-done.29 = f32[4,8,8192]{2,1,0:T(8,128)S(1)} collective-permute-done((f32[4,8,8192]{2,1,0:T(8,128)}, f32[4,8,8192]{2,1,0:T(8,128)S(1)}, u32[]{:S(2)}, u32[]{:S(2)}) %collective-permute-start.29) | collective-permute-done | bytes 1048608 | tf_op jit(solution)/shard_map/ppermute | solution.py:252
  563.4 1.3 fusion.13
  564.8 3.2 collective-permute-start.31
  568.0 1.7 collective-permute-done.24
  569.7 1.2 fusion.24
  570.9 7.0 %collective-permute-done.30 = f32[8,8192]{1,0:T(8,128)S(1)} collective-permute-done((f32[8,8192]{1,0:T(8,128)S(1)}, f32[8,8192]{1,0:T(8,128)S(1)}, u32[]{:S(2)}, u32[]{:S(2)}) %collective-permute-start.30) | collective-permute-done | bytes 262176 | tf_op jit(solution)/shard_map/ppermute | solution.py:256
  578.0 1.1 fusion.17
  579.1 5.2 conditional.1
  579.1 5.2 copy.30
  584.3 5.9 copy.27
  (69 shorter events, 0.5 us)
Async XLA Ops:
  6.5 414.1 %all-gather.3.cloned.1.call-start = ((), (), s32[]{:S(2)}) async-start(), calls=%async_computation.6 | async-start | bytes 8912896 | tf_op jit(solution)/shard_map/all_gather | solution.py:193
  68.3 62.9 %collective-permute-start = (f32[14,128,128]{2,1,0:T(8,128)}, f32[14,128,128]{2,1,0:T(8,128)S(1)}, u32[]{:S(2)}, u32[]{:S(2)}) collective-permute-start(f32[14,128,128]{2,1,0:T(8,128)} %get-tuple-element.54), channel_id=1, source_target_pairs={{0,32},{32,64},{64,96},{96,0},{1,33},{33,65},{65,97},{97,1},{2,34}... | collective-permute-start | bytes 2752520 | tf_op jit(solution)/shard_map/ppermute | solution.py:220
  70.0 61.1 %collective-permute-start.2 = (f32[14,128,128]{2,1,0:T(8,128)}, f32[14,128,128]{2,1,0:T(8,128)S(1)}, u32[]{:S(2)}, u32[]{:S(2)}) collective-permute-start(f32[14,128,128]{2,1,0:T(8,128)} %get-tuple-element.55), channel_id=1, source_target_pairs={{0,96},{32,0},{64,32},{96,64},{1,97},{33,1},{65,33},{97,65},{2,98}... | collective-permute-start | bytes 2752520 | tf_op jit(solution)/shard_map/ppermute | solution.py:220
  129.0 60.8 %collective-permute-start.1 = (f32[14,128,128]{2,1,0:T(8,128)}, f32[14,128,128]{2,1,0:T(8,128)S(1)}, u32[]{:S(2)}, u32[]{:S(2)}) collective-permute-start(f32[14,128,128]{2,1,0:T(8,128)} %get-tuple-element.51), channel_id=1, source_target_pairs={{0,64},{32,96},{64,0},{96,32},{1,65},{33,97},{65,1},{97,33},{2,66}... | collective-permute-start | bytes 2752520 | tf_op jit(solution)/shard_map/ppermute | solution.py:221
  131.2 113.4 %collective-permute-start.3 = (f32[14,128,128]{2,1,0:T(8,128)}, f32[14,128,128]{2,1,0:T(8,128)}, u32[]{:S(2)}, u32[]{:S(2)}) collective-permute-start(f32[14,128,128]{2,1,0:T(8,128)} %get-tuple-element.53.refs_3_), channel_id=1, source_target_pairs={{0,1},{1,0},{2,3},{3,2},{4,5},{5,4},{6,7},{7,6},{8,9},{9,8},{10,11... | collective-permute-start | bytes 2752520 | tf_op jit(solution)/shard_map/ppermute | solution.py:246
  131.2 0.9 copy-start.2
  132.1 1.0 copy-start.4
  186.5 234.2 %copy-start.3 = (f32[14,128,128]{2,1,0:T(8,128)S(1)}, f32[14,128,128]{2,1,0:T(8,128)}, u32[]{:S(2)}) copy-start(f32[14,128,128]{2,1,0:T(8,128)} %copy-done.2) | copy-start | bytes 2752516
  186.5 234.2 %copy-start.5 = (f32[14,128,128]{2,1,0:T(8,128)S(1)}, f32[14,128,128]{2,1,0:T(8,128)}, u32[]{:S(2)}) copy-start(f32[14,128,128]{2,1,0:T(8,128)} %copy-done.4) | copy-start | bytes 2752516
  186.5 58.6 %collective-permute-start.7 = (f32[13,128,128]{2,1,0:T(8,128)}, f32[13,128,128]{2,1,0:T(8,128)}, u32[]{:S(2)}, u32[]{:S(2)}) collective-permute-start(f32[13,128,128]{2,1,0:T(8,128)} %get-tuple-element.57), channel_id=1, source_target_pairs={{0,32},{32,64},{64,96},{96,0},{1,33},{33,65},{65,97},{97,1},{2,34}... | collective-permute-start | bytes 2555912 | tf_op jit(solution)/shard_map/ppermute | solution.py:220
  187.3 57.9 %collective-permute-start.9 = (f32[13,128,128]{2,1,0:T(8,128)}, f32[13,128,128]{2,1,0:T(8,128)}, u32[]{:S(2)}, u32[]{:S(2)}) collective-permute-start(f32[13,128,128]{2,1,0:T(8,128)} %get-tuple-element.59), channel_id=1, source_target_pairs={{0,96},{32,0},{64,32},{96,64},{1,97},{33,1},{65,33},{97,65},{2,98}... | collective-permute-start | bytes 2555912 | tf_op jit(solution)/shard_map/ppermute | solution.py:220
  189.8 1.0 copy-start
  244.2 176.4 %copy-start.1 = (f32[14,128,128]{2,1,0:T(8,128)S(1)}, f32[14,128,128]{2,1,0:T(8,128)}, u32[]{:S(2)}) copy-start(f32[14,128,128]{2,1,0:T(8,128)} %copy-done) | copy-start | bytes 2752516
  244.2 22.7 %collective-permute-start.8 = (f32[13,128,128]{2,1,0:T(8,128)}, f32[13,128,128]{2,1,0:T(8,128)}, u32[]{:S(2)}, u32[]{:S(2)}) collective-permute-start(f32[13,128,128]{2,1,0:T(8,128)} %get-tuple-element.58), channel_id=1, source_target_pairs={{0,64},{32,96},{64,0},{96,32},{1,65},{33,97},{65,1},{97,33},{2,66}... | collective-permute-start | bytes 2555912 | tf_op jit(solution)/shard_map/ppermute | solution.py:221
  244.6 129.8 %collective-permute-start.5 = (f32[14,128,128]{2,1,0:T(8,128)}, f32[14,128,128]{2,1,0:T(8,128)}, u32[]{:S(2)}, u32[]{:S(2)}) collective-permute-start(f32[14,128,128]{2,1,0:T(8,128)} %copy-done), channel_id=1, source_target_pairs={{0,1},{1,0},{2,3},{3,2},{4,5},{5,4},{6,7},{7,6},{8,9},{9,8},{10,11... | collective-permute-start | bytes 2752520 | tf_op jit(solution)/shard_map/ppermute | solution.py:246
  244.6 129.8 %collective-permute-start.4 = (f32[14,128,128]{2,1,0:T(8,128)}, f32[14,128,128]{2,1,0:T(8,128)}, u32[]{:S(2)}, u32[]{:S(2)}) collective-permute-start(f32[14,128,128]{2,1,0:T(8,128)} %copy-done.2), channel_id=1, source_target_pairs={{0,1},{1,0},{2,3},{3,2},{4,5},{5,4},{6,7},{7,6},{8,9},{9,8},{10,11... | collective-permute-start | bytes 2752520 | tf_op jit(solution)/shard_map/ppermute | solution.py:246
  245.1 132.6 %collective-permute-start.6 = (f32[14,128,128]{2,1,0:T(8,128)}, f32[14,128,128]{2,1,0:T(8,128)}, u32[]{:S(2)}, u32[]{:S(2)}) collective-permute-start(f32[14,128,128]{2,1,0:T(8,128)} %copy-done.4), channel_id=1, source_target_pairs={{0,1},{1,0},{2,3},{3,2},{4,5},{5,4},{6,7},{7,6},{8,9},{9,8},{10,11... | collective-permute-start | bytes 2752520 | tf_op jit(solution)/shard_map/ppermute | solution.py:246
  245.2 128.6 %collective-permute-start.10 = (f32[13,128,128]{2,1,0:T(8,128)}, f32[13,128,128]{2,1,0:T(8,128)}, u32[]{:S(2)}, u32[]{:S(2)}) collective-permute-start(f32[13,128,128]{2,1,0:T(8,128)} %get-tuple-element.56.refs_4_), channel_id=1, source_target_pairs={{0,1},{1,0},{2,3},{3,2},{4,5},{5,4},{6,7},{7,6},{8,9},{9,8},{10,11... | collective-permute-start | bytes 2555912 | tf_op jit(solution)/shard_map/ppermute | solution.py:246
  266.9 123.8 %collective-permute-start.11 = (f32[13,128,128]{2,1,0:T(8,128)}, f32[13,128,128]{2,1,0:T(8,128)}, u32[]{:S(2)}, u32[]{:S(2)}) collective-permute-start(f32[13,128,128]{2,1,0:T(8,128)} %collective-permute-done.7.refs_5_.refs_0_), channel_id=1, source_target_pairs={{0,1},{1,0},{2,3},{3,2},{4,5},{5,4},{6,7},{7,6},{8,9},{9,8},{10,11... | collective-permute-start | bytes 2555912 | tf_op jit(solution)/shard_map/ppermute | solution.py:246
  373.8 45.3 %collective-permute-start.13 = (f32[13,128,128]{2,1,0:T(8,128)}, f32[13,128,128]{2,1,0:T(8,128)}, u32[]{:S(2)}, u32[]{:S(2)}) collective-permute-start(f32[13,128,128]{2,1,0:T(8,128)} %collective-permute-done.9.refs_7_.refs_1_), channel_id=1, source_target_pairs={{0,1},{1,0},{2,3},{3,2},{4,5},{5,4},{6,7},{7,6},{8,9},{9,8},{10,11... | collective-permute-start | bytes 2555912 | tf_op jit(solution)/shard_map/ppermute | solution.py:246
  374.4 44.9 %collective-permute-start.14 = (f32[13,128,128]{2,1,0:T(8,128)}, f32[13,128,128]{2,1,0:T(8,128)}, u32[]{:S(2)}, u32[]{:S(2)}) collective-permute-start(f32[13,128,128]{2,1,0:T(8,128)} %get-tuple-element.61), channel_id=1, source_target_pairs={{0,32},{32,64},{64,96},{96,0},{1,33},{33,65},{65,97},{97,1},{2,34}... | collective-permute-start | bytes 2555912 | tf_op jit(solution)/shard_map/ppermute | solution.py:220
  374.4 45.3 %collective-permute-start.16 = (f32[13,128,128]{2,1,0:T(8,128)}, f32[13,128,128]{2,1,0:T(8,128)}, u32[]{:S(2)}, u32[]{:S(2)}) collective-permute-start(f32[13,128,128]{2,1,0:T(8,128)} %get-tuple-element.63), channel_id=1, source_target_pairs={{0,96},{32,0},{64,32},{96,64},{1,97},{33,1},{65,33},{97,65},{2,98}... | collective-permute-start | bytes 2555912 | tf_op jit(solution)/shard_map/ppermute | solution.py:220
  377.7 42.2 %collective-permute-start.15 = (f32[13,128,128]{2,1,0:T(8,128)}, f32[13,128,128]{2,1,0:T(8,128)}, u32[]{:S(2)}, u32[]{:S(2)}) collective-permute-start(f32[13,128,128]{2,1,0:T(8,128)} %get-tuple-element.62), channel_id=1, source_target_pairs={{0,64},{32,96},{64,0},{96,32},{1,65},{33,97},{65,1},{97,33},{2,66}... | collective-permute-start | bytes 2555912 | tf_op jit(solution)/shard_map/ppermute | solution.py:221
  379.2 39.9 %all-to-all-start.3 = ((f32[128,1,41]{2,1,0:T(1,128)}), f32[128,1,41]{2,1,0:T(1,128)S(1)}, u32[]{:S(2)}, u32[]{:S(2)}) async-start(f32[128,1,41]{2,1,0:T(1,128)} %bitcast.13), calls=%async_computation.4 | async-start | bytes 131072 | tf_op jit(solution)/shard_map/all_to_all | solution.py:234
  390.7 57.9 %collective-permute-start.12 = (f32[13,128,128]{2,1,0:T(8,128)}, f32[13,128,128]{2,1,0:T(8,128)}, u32[]{:S(2)}, u32[]{:S(2)}) collective-permute-start(f32[13,128,128]{2,1,0:T(8,128)} %collective-permute-done.8.refs_6_.refs_0_), channel_id=1, source_target_pairs={{0,1},{1,0},{2,3},{3,2},{4,5},{5,4},{6,7},{7,6},{8,9},{9,8},{10,11... | collective-permute-start | bytes 2555912 | tf_op jit(solution)/shard_map/ppermute | solution.py:246
  419.2 57.4 %collective-permute-start.17 = (f32[13,128,128]{2,1,0:T(8,128)}, f32[13,128,128]{2,1,0:T(8,128)}, u32[]{:S(2)}, u32[]{:S(2)}) collective-permute-start(f32[13,128,128]{2,1,0:T(8,128)} %get-tuple-element.60.refs_4_), channel_id=1, source_target_pairs={{0,1},{1,0},{2,3},{3,2},{4,5},{5,4},{6,7},{7,6},{8,9},{9,8},{10,11... | collective-permute-start | bytes 2555912 | tf_op jit(solution)/shard_map/ppermute | solution.py:246
  419.3 57.3 %collective-permute-start.18 = (f32[13,128,128]{2,1,0:T(8,128)}, f32[13,128,128]{2,1,0:T(8,128)}, u32[]{:S(2)}, u32[]{:S(2)}) collective-permute-start(f32[13,128,128]{2,1,0:T(8,128)} %collective-permute-done.14.refs_5_), channel_id=1, source_target_pairs={{0,1},{1,0},{2,3},{3,2},{4,5},{5,4},{6,7},{7,6},{8,9},{9,8},{10,11... | collective-permute-start | bytes 2555912 | tf_op jit(solution)/shard_map/ppermute | solution.py:246
  419.8 56.8 %collective-permute-start.20 = (f32[13,128,128]{2,1,0:T(8,128)}, f32[13,128,128]{2,1,0:T(8,128)}, u32[]{:S(2)}, u32[]{:S(2)}) collective-permute-start(f32[13,128,128]{2,1,0:T(8,128)} %collective-permute-done.16.refs_7_), channel_id=1, source_target_pairs={{0,1},{1,0},{2,3},{3,2},{4,5},{5,4},{6,7},{7,6},{8,9},{9,8},{10,11... | collective-permute-start | bytes 2555912 | tf_op jit(solution)/shard_map/ppermute | solution.py:246
  419.9 56.7 %collective-permute-start.19 = (f32[13,128,128]{2,1,0:T(8,128)}, f32[13,128,128]{2,1,0:T(8,128)}, u32[]{:S(2)}, u32[]{:S(2)}) collective-permute-start(f32[13,128,128]{2,1,0:T(8,128)} %collective-permute-done.15.refs_6_), channel_id=1, source_target_pairs={{0,1},{1,0},{2,3},{3,2},{4,5},{5,4},{6,7},{7,6},{8,9},{9,8},{10,11... | collective-permute-start | bytes 2555912 | tf_op jit(solution)/shard_map/ppermute | solution.py:246
  420.7 1.2 copy-start.6
  421.9 26.8 %copy-start.7 = (f32[13,128,128]{2,1,0:T(8,128)S(1)}, f32[13,128,128]{2,1,0:T(8,128)}, u32[]{:S(2)}) copy-start(f32[13,128,128]{2,1,0:T(8,128)} %get-tuple-element.56.refs_4_) | copy-start | bytes 2555908
  448.6 28.0 %copy-start.8 = (f32[13,128,128]{2,1,0:T(8,128)S(1)}, f32[13,128,128]{2,1,0:T(8,128)}, u32[]{:S(2)}) copy-start(f32[13,128,128]{2,1,0:T(8,128)} %get-tuple-element.60.refs_4_) | copy-start | bytes 2555908
  476.5 102.6 %copy-start.9 = (s32[128,1]{0,1:T(1,128)S(1)}, s32[128,1]{0,1:T(1,128)}, u32[]{:S(2)}) copy-start(s32[128,1]{0,1:T(1,128)} %param.9) | copy-start | bytes 1540
  476.5 102.6 %copy-start.10 = (s32[128]{0:T(128)S(1)}, s32[128]{0:T(128)}, u32[]{:S(2)}) copy-start(s32[128]{0:T(128)} %param.11) | copy-start | bytes 1540
  476.5 102.6 %copy-start.11 = (s32[128]{0:T(128)S(1)}, s32[128]{0:T(128)}, u32[]{:S(2)}) copy-start(s32[128]{0:T(128)} %param.10) | copy-start | bytes 1540
  493.9 26.7 %collective-permute-start.21 = (f32[4,8,8192]{2,1,0:T(8,128)}, f32[4,8,8192]{2,1,0:T(8,128)S(1)}, u32[]{:S(2)}, u32[]{:S(2)}) collective-permute-start(f32[4,8,8192]{2,1,0:T(8,128)} %get-tuple-element.65), channel_id=1, source_target_pairs={{0,2},{1,3},{2,4},{3,5},{4,6},{5,7},{6,0},{7,1},{8,10},{9,11},{10,... | collective-permute-start | bytes 3145736 | tf_op jit(solution)/shard_map/ppermute | solution.py:251
  495.1 49.5 %collective-permute-start.22 = (f32[4,8,8192]{2,1,0:T(8,128)}, f32[4,8,8192]{2,1,0:T(8,128)}, u32[]{:S(2)}, u32[]{:S(2)}) collective-permute-start(f32[4,8,8192]{2,1,0:T(8,128)} %get-tuple-element.66), channel_id=1, source_target_pairs={{0,6},{1,7},{2,0},{3,1},{4,2},{5,3},{6,4},{7,5},{8,14},{9,15},{10,... | collective-permute-start | bytes 3145736 | tf_op jit(solution)/shard_map/ppermute | solution.py:251
  497.2 47.5 %collective-permute-start.23 = (f32[4,8,8192]{2,1,0:T(8,128)}, f32[4,8,8192]{2,1,0:T(8,128)}, u32[]{:S(2)}, u32[]{:S(2)}) collective-permute-start(f32[4,8,8192]{2,1,0:T(8,128)} %get-tuple-element.67), channel_id=1, source_target_pairs={{0,4},{1,5},{2,6},{3,7},{4,0},{5,1},{6,2},{7,3},{8,12},{9,13},{10,... | collective-permute-start | bytes 3145736 | tf_op jit(solution)/shard_map/ppermute | solution.py:251
  499.5 50.1 %collective-permute-start.27 = (f32[4,8,8192]{2,1,0:T(8,128)}, f32[4,8,8192]{2,1,0:T(8,128)S(1)}, u32[]{:S(2)}, u32[]{:S(2)}) collective-permute-start(f32[4,8,8192]{2,1,0:T(8,128)} %get-tuple-element.69), channel_id=1, source_target_pairs={{0,8},{1,9},{2,10},{3,11},{4,12},{5,13},{6,14},{7,15},{8,16},{9,17... | collective-permute-start | bytes 3145736 | tf_op jit(solution)/shard_map/ppermute | solution.py:252
  501.7 48.0 %collective-permute-start.28 = (f32[4,8,8192]{2,1,0:T(8,128)}, f32[4,8,8192]{2,1,0:T(8,128)S(1)}, u32[]{:S(2)}, u32[]{:S(2)}) collective-permute-start(f32[4,8,8192]{2,1,0:T(8,128)} %get-tuple-element.70), channel_id=1, source_target_pairs={{0,24},{1,25},{2,26},{3,27},{4,28},{5,29},{6,30},{7,31},{8,0},{9,1... | collective-permute-start | bytes 3145736 | tf_op jit(solution)/shard_map/ppermute | solution.py:252
  520.6 42.8 %collective-permute-start.29 = (f32[4,8,8192]{2,1,0:T(8,128)}, f32[4,8,8192]{2,1,0:T(8,128)S(1)}, u32[]{:S(2)}, u32[]{:S(2)}) collective-permute-start(f32[4,8,8192]{2,1,0:T(8,128)} %get-tuple-element.71), channel_id=1, source_target_pairs={{0,16},{1,17},{2,18},{3,19},{4,20},{5,21},{6,22},{7,23},{8,24},{9,... | collective-permute-start | bytes 3145736 | tf_op jit(solution)/shard_map/ppermute | solution.py:252
  546.4 23.3 %collective-permute-start.24 = (f32[8,8192]{1,0:T(8,128)S(1)}, f32[8,8192]{1,0:T(8,128)S(1)}, u32[]{:S(2)}, u32[]{:S(2)}) collective-permute-start(f32[8,8192]{1,0:T(8,128)S(1)} %get-tuple-element.111), channel_id=1, source_target_pairs={{0,8},{1,9},{2,10},{3,11},{4,12},{5,13},{6,14},{7,15},{8,16},{9,17... | collective-permute-start | bytes 786440 | tf_op jit(solution)/shard_map/ppermute | solution.py:255
  546.6 23.1 %collective-permute-start.25 = (f32[8,8192]{1,0:T(8,128)S(1)}, f32[8,8192]{1,0:T(8,128)S(1)}, u32[]{:S(2)}, u32[]{:S(2)}) collective-permute-start(f32[8,8192]{1,0:T(8,128)S(1)} %get-tuple-element.113), channel_id=1, source_target_pairs={{0,24},{1,25},{2,26},{3,27},{4,28},{5,29},{6,30},{7,31},{8,0},{9,1... | collective-permute-start | bytes 786440 | tf_op jit(solution)/shard_map/ppermute | solution.py:255
  549.7 20.0 %collective-permute-start.26 = (f32[8,8192]{1,0:T(8,128)S(1)}, f32[8,8192]{1,0:T(8,128)S(1)}, u32[]{:S(2)}, u32[]{:S(2)}) collective-permute-start(f32[8,8192]{1,0:T(8,128)S(1)} %get-tuple-element.112), channel_id=1, source_target_pairs={{0,16},{1,17},{2,18},{3,19},{4,20},{5,21},{6,22},{7,23},{8,24},{9,... | collective-permute-start | bytes 786440 | tf_op jit(solution)/shard_map/ppermute | solution.py:255
  564.7 13.3 %collective-permute-start.30 = (f32[8,8192]{1,0:T(8,128)S(1)}, f32[8,8192]{1,0:T(8,128)S(1)}, u32[]{:S(2)}, u32[]{:S(2)}) collective-permute-start(f32[8,8192]{1,0:T(8,128)S(1)} %get-tuple-element.114), channel_id=1, source_target_pairs={{0,2},{1,3},{2,4},{3,5},{4,6},{5,7},{6,0},{7,1},{8,10},{9,11},{10,... | collective-permute-start | bytes 786440 | tf_op jit(solution)/shard_map/ppermute | solution.py:256
  564.8 13.2 %collective-permute-start.31 = (f32[8,8192]{1,0:T(8,128)S(1)}, f32[8,8192]{1,0:T(8,128)S(1)}, u32[]{:S(2)}, u32[]{:S(2)}) collective-permute-start(f32[8,8192]{1,0:T(8,128)S(1)} %get-tuple-element.116), channel_id=1, source_target_pairs={{0,6},{1,7},{2,0},{3,1},{4,2},{5,3},{6,4},{7,5},{8,14},{9,15},{10,... | collective-permute-start | bytes 786440 | tf_op jit(solution)/shard_map/ppermute | solution.py:256
  569.7 8.3 %collective-permute-start.32 = (f32[8,8192]{1,0:T(8,128)S(1)}, f32[8,8192]{1,0:T(8,128)S(1)}, u32[]{:S(2)}, u32[]{:S(2)}) collective-permute-start(f32[8,8192]{1,0:T(8,128)S(1)} %get-tuple-element.115), channel_id=1, source_target_pairs={{0,4},{1,5},{2,6},{3,7},{4,0},{5,1},{6,2},{7,3},{8,12},{9,13},{10,... | collective-permute-start | bytes 786440 | tf_op jit(solution)/shard_map/ppermute | solution.py:256
Sparse Core Ops, SparseCore 0:
  9.5 73.3 all-gather.2

commit v2 on v1

v2 whole, which is shorter than its diff:
```python
import functools

import jax
import jax.numpy as jnp
from jax import lax
from jax.experimental import pallas as pl
from jax.experimental.pallas import tpu as pltpu
from jax.sharding import PartitionSpec as P

TILE = 128
SLOTS = 40
FIRST = 30
VMEM = 60 * 1024 * 1024
AXES = ("grp", "inner")


def slow_part(amplitude, integrals, tile_owner, tile_row, tile_col):
    n_grp, n_inner = lax.axis_size("grp"), lax.axis_size("inner")
    devices = n_grp * n_inner
    count, size = integrals.shape[:2]
    blocks = amplitude.shape[1] // size
    per_dev = blocks // n_inner
    capacity = max(2, 2 * count // devices)
    owners = tile_owner[:, 0]
    order = jnp.arange(count, dtype=jnp.int32)
    same = (owners[:, None] == owners[None, :]) & (order[None, :] < order[:, None])
    slot = owners * capacity + jnp.sum(same.astype(jnp.int32), axis=1)
    position = (tile_row * blocks + tile_col).astype(jnp.float32)
    tiles = jnp.zeros((devices * capacity, size, size), jnp.float32).at[slot].set(integrals)
    place = jnp.zeros((devices * capacity,), jnp.float32).at[slot].set(position)
    tiles, place = (
        lax.all_to_all(tiles, AXES, split_axis=0, concat_axis=0, tiled=True),
        lax.all_to_all(place, AXES, split_axis=0, concat_axis=0, tiled=True),
    )
    dense = jnp.zeros((per_dev * blocks, size, size), jnp.float32).at[place.astype(jnp.int32)].add(tiles)
    dense = dense.reshape(per_dev, blocks, size, size).transpose(0, 2, 1, 3).reshape(per_dev * size, blocks * size)
    slab = lax.all_to_all(amplitude, "inner", split_axis=1, concat_axis=0, tiled=True)
    return lax.psum_scatter(
        jnp.dot(slab, dense, precision=lax.Precision.HIGHEST, preferred_element_type=jnp.float32),
        "inner",
        scatter_dimension=0,
        tiled=True,
    )


def pack_kernel(spans, total, index, tiles, *refs):
    outs, sems = refs[: len(spans)], refs[-1]
    for at, (which, lo, hi) in enumerate(spans):

        def issue(k, _):
            pltpu.make_async_copy(tiles.at[index[which * total + lo + k]], outs[at].at[k], sems.at[at]).start()
            return 0

        lax.fori_loop(0, hi - lo, issue, 0)
    for at, (_, lo, hi) in enumerate(spans):
        pltpu.make_async_copy(tiles.at[pl.ds(0, hi - lo)], outs[at], sems.at[at]).wait()


def pack(integrals, index, spans, total):
    return pl.pallas_call(
        functools.partial(pack_kernel, spans, total),
        out_shape=[jax.ShapeDtypeStruct((hi - lo, TILE, TILE), jnp.float32) for _, lo, hi in spans],
        in_specs=[pl.BlockSpec(memory_space=pltpu.SMEM), pl.BlockSpec(memory_space=pl.ANY)],
        out_specs=[pl.BlockSpec(memory_space=pltpu.VMEM)] * len(spans),
        scratch_shapes=[pltpu.SemaphoreType.DMA((len(spans),))],
        compiler_params=pltpu.CompilerParams(vmem_limit_bytes=VMEM),
        cost_estimate=pl.CostEstimate(flops=0, bytes_accessed=1000, transcendentals=0),
    )(index, integrals)


def add_kernel(one, two, out):
    out[...] = one[...] + two[...]


def add(one, two):
    return pl.pallas_call(add_kernel, out_shape=jax.ShapeDtypeStruct(one.shape, one.dtype))(one, two)


def gate_kernel(*refs):
    pass


def gate(value, *after):
    any_spec = pl.BlockSpec(memory_space=pl.ANY)
    return pl.pallas_call(
        gate_kernel,
        out_shape=jax.ShapeDtypeStruct(value.shape, value.dtype),
        in_specs=[any_spec] * (1 + len(after)),
        out_specs=any_spec,
        input_output_aliases={0: 0},
    )(value, *after)


def split(value):
    high = value.astype(jnp.bfloat16)
    return high, (value - high.astype(jnp.float32)).astype(jnp.bfloat16)


def ladder_kernel(counts, blocks, has_acc, last, *refs):
    refs, lists = list(refs), len(counts)
    code, where, amp = refs[:3]
    del refs[:3]
    acc_in = refs.pop(0) if has_acc else None
    tiles = refs[:lists]
    del refs[:lists]
    acc_out = None if last else refs.pop(0)
    parts = [refs.pop(0) for _ in range(8)] if last else []
    tile_v = refs[:lists]
    amp_v, acc_v, amp_sem, acc_sem, tile_sem, out_sem = refs[lists:]

    z, x = where[0], where[1]
    for sx in range(4):
        for sz in range(4):
            source = lax.rem(z + sz, 4) * 4 + lax.rem(x + sx, 4)
            pltpu.make_async_copy(amp.at[source], amp_v.at[sx * 4 + sz], amp_sem).start()
    if has_acc:
        acc_copy = pltpu.make_async_copy(acc_in, acc_v, acc_sem)
        acc_copy.start()
    copies = [pltpu.make_async_copy(tiles[k], tile_v[k], tile_sem.at[k]) for k in range(lists)]
    for copy in copies:
        copy.start()
    if has_acc:
        acc_copy.wait()
    else:
        acc_v[...] = jnp.zeros_like(acc_v)
    pltpu.make_async_copy(amp, amp_v, amp_sem).wait()

    for k in range(lists):
        copies[k].wait()
        base = sum(counts[:k])

        def pair(j, _):
            places = [code[base + 2 * j], code[base + 2 * j + 1]]

            @pl.when(jnp.maximum(*places) >= 0)
            def _():
                terms = []
                for half, place in enumerate(places):
                    held = jnp.maximum(place, 0)
                    row = pl.multiple_of((held // blocks) * TILE, TILE)
                    col = pl.multiple_of(lax.rem(held, blocks) * TILE, TILE)
                    a_hi, a_lo = split(amp_v[:, :, pl.ds(row, TILE)].reshape(16 * 8, TILE))
                    t_hi, t_lo = split(jnp.where(place >= 0, tile_v[k][2 * j + half], 0.0))
                    left = jnp.concatenate([a_hi, a_lo], axis=1)
                    right = jnp.concatenate([t_hi, t_lo], axis=1)
                    both = jnp.dot(left, jnp.concatenate([right, right], axis=0), preferred_element_type=jnp.float32)
                    terms.append((col, (both[:, :TILE] + both[:, TILE:]).reshape(4, 4, 8, TILE)))
                for col, term in terms:
                    acc_v[:, :, :, pl.ds(col, TILE)] += term

            return 0

        lax.fori_loop(0, counts[k] // 2, pair, 0)

    if last:
        done, half = [], blocks * TILE // 2
        for s in range(4):
            done.append(pltpu.make_async_copy(acc_v.at[s, :, :, pl.ds(0, half)], parts[s], out_sem.at[s]))
            done.append(pltpu.make_async_copy(acc_v.at[:, s, :, pl.ds(half, half)], parts[4 + s], out_sem.at[4 + s]))
    else:
        done = [pltpu.make_async_copy(acc_v, acc_out, out_sem.at[0])]
    for copy in done:
        copy.start()
    for copy in done:
        copy.wait()


def ladder(code, where, amp, acc, tiles, last, blocks, guess):
    counts = tuple(t.shape[0] for t in tiles)
    any_spec, smem = pl.BlockSpec(memory_space=pl.ANY), pl.BlockSpec(memory_space=pltpu.SMEM)
    if last:
        shapes = [jax.ShapeDtypeStruct((4, 8, blocks * TILE // 2), jnp.float32)] * 8
    else:
        shapes = [jax.ShapeDtypeStruct((4, 4, 8, blocks * TILE), jnp.float32)]
    given = [code, where, amp] + ([] if acc is None else [acc]) + list(tiles)
    return pl.pallas_call(
        functools.partial(ladder_kernel, counts, blocks, acc is not None, last),
        out_shape=shapes,
        in_specs=[smem, smem] + [any_spec] * (len(given) - 2),
        out_specs=[any_spec] * len(shapes),
        scratch_shapes=[
            *[pltpu.VMEM((n, TILE, TILE), jnp.float32) for n in counts],
            pltpu.VMEM((16, 8, blocks * TILE), jnp.float32),
            pltpu.VMEM((4, 4, 8, blocks * TILE), jnp.float32),
            pltpu.SemaphoreType.DMA,
            pltpu.SemaphoreType.DMA,
            pltpu.SemaphoreType.DMA((len(tiles),)),
            pltpu.SemaphoreType.DMA((9,)),
        ],
        compiler_params=pltpu.CompilerParams(vmem_limit_bytes=VMEM),
        cost_estimate=pl.CostEstimate(flops=0, bytes_accessed=guess, transcendentals=0),
    )(*given)


def per_device(amplitude, integrals, tile_owner, tile_row, tile_col):
    n_grp, n_inner = lax.axis_size("grp"), lax.axis_size("inner")
    devices = n_grp * n_inner
    rows, width = amplitude.shape
    count = integrals.shape[0]
    blocks = width // TILE
    per_dev = blocks // n_inner
    total = SLOTS
    grp, inner = lax.axis_index("grp"), lax.axis_index("inner")
    z, x, core = inner // 8, (inner // 2) % 4, inner % 2

    def at(z, x, core):
        return (z % 4) * 8 + (x % 4) * 2 + core

    every = [(a, b, c) for a in range(4) for b in range(4) for c in range(2)]
    along_x = {s: [(at(a, b, c), at(a, b + s, c)) for a, b, c in every] for s in (1, 2, 3)}
    along_z = {s: [(at(a, b, c), at(a + s, b, c)) for a, b, c in every] for s in (1, 2, 3)}
    along_y = {s: [(i, (i + s) % n_grp) for i in range(n_grp)] for s in (1, 2, 3)}
    across = [(i, i ^ 1) for i in range(n_inner)]
    same_core = [[at(a, b, c) for a in range(4) for b in range(4)] for c in range(2)]

    amp = lax.all_gather(amplitude, "inner", axis=0, axis_index_groups=same_core)

    owners = tile_owner[:, 0]
    slab = owners // n_inner
    step = (slab - grp + n_grp) % n_grp
    order = jnp.arange(count, dtype=jnp.int32)
    key = tile_col * count + order
    ahead = (slab[:, None] == slab[None, :]) & (key[None, :] < key[:, None])
    rank = jnp.sum(ahead.astype(jnp.int32), axis=1)
    fits = rank < total
    code = ((owners % n_inner) * per_dev + tile_row) * blocks + tile_col
    slots = jnp.arange(n_grp * total, dtype=jnp.int32)[:, None]
    mine = jnp.where(fits, step * total + rank, -1)[None, :] == slots
    index = jnp.sum(jnp.where(mine, order[None, :], 0), axis=1)
    theirs = jnp.where(fits, slab * total + rank, -1)[None, :] == slots
    codes = jnp.sum(jnp.where(theirs, code[None, :] + 1, 0), axis=1) - 1
    left_over = jnp.sum((~fits).astype(jnp.int32))

    where = jnp.stack([z, x]).astype(jnp.int32)

    def finish(parts):
        one, two = parts[:4], parts[4:]
        r1 = [lax.ppermute(one[s], "inner", along_x[s]) for s in (1, 3, 2)]
        r2 = [lax.ppermute(two[s], "inner", along_z[s]) for s in (1, 3, 2)]
        s1 = [one[0][q] + r1[0][q] + r1[1][q] + r1[2][q] for q in range(4)]
        s2 = [two[0][q] + r2[0][q] + r2[1][q] + r2[2][q] for q in range(4)]
        f1 = [lax.ppermute(s1[s], "inner", along_z[s]) for s in (1, 3, 2)]
        f2 = [lax.ppermute(s2[s], "inner", along_x[s]) for s in (1, 3, 2)]
        return [s1[0] + f1[0] + f1[1] + f1[2], s2[0] + f2[0] + f2[1] + f2[2]]

    p1, p3 = pack(integrals, index, ((1, 0, total), (3, 0, total)), total)
    r1, r3 = lax.ppermute(p1, "grp", along_y[1]), lax.ppermute(p3, "grp", along_y[3])
    p2, p4, p0 = pack(integrals, index, ((2, 0, FIRST), (2, FIRST, total), (0, 0, total)), total)
    r2, r4 = lax.ppermute(p2, "grp", along_y[2]), lax.ppermute(p4, "grp", along_y[2])
    codes, _ = lax.optimization_barrier((codes, p4))
    note = jnp.concatenate(
        [
            jnp.broadcast_to(codes.reshape(n_grp, 1, total), (n_grp, n_inner, total)),
            jnp.broadcast_to(left_over, (n_grp, n_inner, 1)),
        ],
        axis=2,
    ).astype(jnp.float32)
    note = lax.all_to_all(note.reshape(devices, total + 1), AXES, split_axis=0, concat_axis=0, tiled=True)
    overflow = jnp.sum(note[:, total]) > 0.5
    note = note[:, :total].reshape(n_grp, n_inner // 2, 2, total)
    note = lax.dynamic_index_in_dim(note, inner // 2, axis=1, keepdims=False)
    note = jnp.stack([lax.dynamic_index_in_dim(note, (grp - s + n_grp) % n_grp, axis=0, keepdims=False) for s in range(4)])
    note = jnp.stack([lax.dynamic_index_in_dim(note, core, axis=1, keepdims=False), lax.dynamic_index_in_dim(note, 1 - core, axis=1, keepdims=False)])
    note = note.astype(jnp.int32)

    def codes_of(steps, lo, hi):
        return jnp.concatenate([note[side, s, lo:hi] for side in range(2) for s in steps])

    def with_other(tiles):
        return [*tiles, *[lax.ppermute(t, "inner", across) for t in tiles]]

    (acc,) = ladder(codes_of((0, 1, 3), 0, total), where, amp, None, with_other([p0, gate(r1, note), gate(r3, note)]), False, blocks, 2 * 10**8)
    (acc,) = ladder(codes_of((2,), 0, FIRST), where, amp, acc, with_other([gate(r2, acc)]), False, blocks, 10**8)
    parts = ladder(codes_of((2,), FIRST, total), where, amp, acc, with_other([gate(r4, acc)]), True, blocks, 10**8)
    pieces = finish(parts)
    out = jnp.concatenate(pieces, axis=1)

    def with_rest(out):
        rest = jnp.where(fits[:, None, None], 0.0, integrals)
        return add(out, slow_part(amplitude, rest, tile_owner, tile_row, tile_col))

    return lax.cond(overflow, with_rest, lambda out: out, out)


def solution(mesh):
    placed = (P(AXES, None), P(AXES, None, None), P(AXES, None), P(AXES), P(AXES))
    return jax.shard_map(per_device, mesh=mesh, in_specs=placed, out_specs=P(AXES, None), check_vma=False)
```

time: 607 us -> 272 us (0.45); the launches traced: 597 us -> 271 us
  Pallas kernels: 400 us -> 73.2 us
  waiting for transfers between devices: 90.2 us -> 129 us
  starting transfers between devices: 65.1 us -> 34.8 us
  local copies, waits for them, and re-layouts: 15.6 us -> 7.5 us
    pallas_call x9, Pallas kernels: 400 us -> 73.2 us  [the longest x3 61.2 us: ladder(): pl.pallas_call(functools.partial(ladder_kernel, counts, blocks, acc is no...]
    ppermute x27 -> x19, waiting for transfers between devices: 61.2 us -> 83.9 us  [the longest x3 41.2 us: finish(): r1 = [lax.ppermute(one[s], 'inner', along_x[s]) for s in (1, 3, 2)]]
    ppermute x27 -> x19, starting transfers between devices: 43.9 us -> 21.6 us  [the longest x3 4.76 us: finish(): r1 = [lax.ppermute(one[s], 'inner', along_x[s]) for s in (1, 3, 2)]]
    all_to_all x1, waiting for transfers between devices: 28.3 us -> 44.7 us  [per_device(): lax.all_to_all(note.reshape(devices, total + 1), AXES, split_axis=0, conc...]
  transfers between devices with their start and end apart: 35 -> 23, of which waited for: 6 -> 12; matrix products, arithmetic and copies ran while one was open for 2% -> 4% of each run, Pallas kernels for 64% -> 23%
where the time goes in v2:
time: 272 us; the launch traced here: 271 us
  waiting for transfers between devices  129 us (47%)
  Pallas kernels  73.2 us (27%)
  starting transfers between devices  34.8 us (13%)
  between operations  14.4 us (5%)
  other arithmetic  12 us (4%)
  local copies, waits for them, and re-layouts  7.5 us (3%)
    pallas_call x3, Pallas kernels, ladder(): pl.pallas_call(functools.partial(ladder_kernel, counts, blocks, acc is no...  61.2 us
    all_to_all x1, waiting for transfers between devices, per_device(): lax.all_to_all(note.reshape(devices, total + 1), AXES, split_axis=0, conc...  44.7 us
    ppermute x3, waiting for transfers between devices, finish(): r1 = [lax.ppermute(one[s], 'inner', along_x[s]) for s in (1, 3, 2)]  41.2 us
    ppermute x3, waiting for transfers between devices, finish(): r2 = [lax.ppermute(two[s], 'inner', along_z[s]) for s in (1, 3, 2)]  19.6 us
    pallas_call x2, Pallas kernels, pack(): pl.pallas_call(functools.partial(pack_kernel, spans, total), out_shape=[j...  12 us
    all_to_all x1, starting transfers between devices, per_device(): lax.all_to_all(note.reshape(devices, total + 1), AXES, split_axis=0, conc...  9.86 us
    ppermute x5, waiting for transfers between devices, with_other(): return [*tiles, *[lax.ppermute(t, 'inner', across) for t in tiles]]  7.25 us
    unnamed x20, local copies, waits for them, and re-layouts  6.67 us
  transfers between devices with their start and end apart: 23, of which 12 were waited for; matrix products, arithmetic and copies ran while one was open for 4% of the time, Pallas kernels for 23%

profile of v2, /device:TPU:0, one launch (start us, length us, event | category | flops | bytes accessed | tf_op | source)
XLA Modules:
  0.0 271.4 jit_solution(1951534417903347480)
XLA Ops:
  6.5 0.7 all-gather.3.cloned.1.call-update
  7.3 0.7 fusion.36
  7.9 0.7 and_select_fusion.2
  8.6 0.2 convert_reduce_fusion.2
  8.8 0.7 fusion.33
  9.5 0.7 select_reduce_fusion
  10.2 5.9 %shard_map.58 = (f32[40,128,128]{2,1,0:T(8,128)}, f32[40,128,128]{2,1,0:T(8,128)}) custom-call(s32[160]{0:T(256)} %get-tuple-element.87.index, f32[128,128,128]{2,1,0:T(8,128)} %tiles.3), custom_call_target="tpu_custom_call" | custom-call | bytes 1000 | tf_op jit(solution)/shard_map/pallas_call | solution.py:60
  16.1 1.6 collective-permute-start
  17.8 1.7 collective-permute-start.1
  19.5 6.1 %shard_map.57 = (f32[30,128,128]{2,1,0:T(8,128)}, f32[10,128,128]{2,1,0:T(8,128)}, f32[40,128,128]{2,1,0:T(8,128)}) custom-call(s32[160]{0:T(256)} %get-tuple-element.87.index, f32[128,128,128]{2,1,0:T(8,128)} %tiles.3), custom_call_target="tpu_custom_call" | custom-call | bytes 1000 | tf_op jit(solution)/shard_map/pallas_call | solution.py:60
  25.6 0.1 broadcast_in_dim.59
  25.7 1.3 pad_convert_fusion
  27.0 9.9 %all-to-all-start.3 = ((f32[128,1,41]{2,1,0:T(1,128)}), f32[128,1,41]{2,1,0:T(1,128)S(1)}, u32[]{:S(2)}, u32[]{:S(2)}) async-start(f32[128,1,41]{2,1,0:T(1,128)} %bitcast.13), calls=%async_computation.4 | async-start | bytes 131072 | tf_op jit(solution)/shard_map/all_to_all | solution.py:258
  36.9 0.1 collective-permute-start.2
  37.1 44.7 %all-to-all-done.3 = f32[128,1,41]{2,1,0:T(1,128)S(1)} async-done(((f32[128,1,41]{2,1,0:T(1,128)}), f32[128,1,41]{2,1,0:T(1,128)S(1)}, u32[]{:S(2)}, u32[]{:S(2)}) %all-to-all-start.3) | async-done | bytes 21024 | tf_op jit(solution)/shard_map/all_to_all | solution.py:258
  81.8 0.6 maximum_convert_fusion.refs_1_
  82.4 1.5 copy-done
  83.9 0.5 collective-permute-start.4
  84.4 1.8 collective-permute-start.5
  86.2 0.6 pad_add_fusion.1.refs_1_
  86.8 0.7 concatenate.21.refs_0_
  87.5 0.2 collective-permute-done.3.refs_7_
  87.6 3.7 %collective-permute-done.4.refs_8_ = f32[40,128,128]{2,1,0:T(8,128)} collective-permute-done((f32[40,128,128]{2,1,0:T(8,128)}, f32[40,128,128]{2,1,0:T(8,128)}, u32[]{:S(2)}, u32[]{:S(2)}) %collective-permute-start.4) | collective-permute-done | bytes 2621472 | tf_op jit(solution)/shard_map/ppermute | solution.py:270
  91.4 33.1 %shard_map.61.refs_1_.refs_3_ = f32[4,4,8,16384]{3,2,1,0:T(8,128)} custom-call(s32[240]{0:T(256)} %concatenate.21.refs_0_, s32[2]{0:T(128)} %pad_add_fusion.1.refs_1_, f32[16,8,16384]{2,1,0:T(8,128)} %bitcast.111, f32[40,128,128]{2,1,0:T(8,128)} %get-tuple-element.46.refs_3_, f32[40,128,128]{2,1,0:T(8,128)} %shard_map.59.refs_4_, ...), custom_call_target="tpu_custom_call" | custom-call | bytes 200000000 | tf_op jit(solution)/shard_map/pallas_call | solution.py:176
  124.5 6.3 %collective-permute-done.5.refs_0_ = f32[30,128,128]{2,1,0:T(8,128)S(1)} collective-permute-done((f32[30,128,128]{2,1,0:T(8,128)}, f32[30,128,128]{2,1,0:T(8,128)S(1)}, u32[]{:S(2)}, u32[]{:S(2)}) %collective-permute-start.5) | collective-permute-done | bytes 1966112 | tf_op jit(solution)/shard_map/ppermute | solution.py:249
  130.8 1.3 copy-done.1
  132.1 1.8 collective-permute-start.7
  133.9 0.6 pad_add_fusion.2.refs_0_
  134.5 1.8 collective-permute-done.6.refs_5_
  136.3 1.3 copy-done.4
  137.7 17.1 %shard_map.63.refs_1_.refs_3_ = f32[4,4,8,16384]{3,2,1,0:T(8,128)} custom-call(s32[60]{0:T(128)} %pad_add_fusion.2.refs_0_, s32[2]{0:T(128)} %pad_add_fusion.1.refs_1_, f32[16,8,16384]{2,1,0:T(8,128)} %bitcast.112, f32[4,4,8,16384]{3,2,1,0:T(8,128)} %shard_map.61.refs_1_.refs_3_, f32[30,128,128]{2,1,0:T(8,128)} %shard_map.62.refs_4_, f32[30,128,128]{2,1,0:T(8,128)} %copy-done.4), custom_call_target="tpu_custom_call" | custom-call | bytes 100000000 | tf_op jit(solution)/shard_map/pallas_call | solution.py:176
  154.8 0.8 copy-done.2
  155.6 0.1 collective-permute-start.8
  155.8 0.1 slice_bitcast_fusion.9
  155.8 0.6 pad_add_fusion.refs_0_
  156.4 1.5 collective-permute-done.8.refs_5_
  157.9 0.9 copy-done.5
  158.9 10.9 %shard_map.65 = (f32[4,8,8192]{2,1,0:T(8,128)}, f32[4,8,8192]{2,1,0:T(8,128)}, f32[4,8,8192]{2,1,0:T(8,128)}, f32[4,8,8192]{2,1,0:T(8,128)}, f32[4,8,8192]{2,1,0...) custom-call(s32[20]{0:T(128)} %pad_add_fusion.refs_0_, s32[2]{0:T(128)} %pad_add_fusion.1.refs_1_, ...), custom_call_target="tpu_custom_call" | custom-call | bytes 100000000 | tf_op jit(solution)/shard_map/pallas_call | solution.py:176
  169.8 0.0 copy-start.8
  169.8 2.8 %collective-permute-start.10 = (f32[4,8,8192]{2,1,0:T(8,128)}, f32[4,8,8192]{2,1,0:T(8,128)S(1)}, u32[]{:S(2)}, u32[]{:S(2)}) collective-permute-start(f32[4,8,8192]{2,1,0:T(8,128)} %get-tuple-element.52), channel_id=1, source_target_pairs={{0,6},{1,7},{2,0},{3,1},{4,2},{5,3},{6,4},{7,5},{8,14},{9,15},{10,... | collective-permute-start | bytes 3145736 | tf_op jit(solution)/shard_map/ppermute | solution.py:238
  172.6 0.9 collective-permute-start.11
  173.5 1.1 collective-permute-start.9
  174.6 0.7 slice_reduce_fusion
  175.9 0.6 collective-permute-start.15
  176.5 2.7 %collective-permute-start.16 = (f32[4,8,8192]{2,1,0:T(8,128)}, f32[4,8,8192]{2,1,0:T(8,128)S(1)}, u32[]{:S(2)}, u32[]{:S(2)}) collective-permute-start(f32[4,8,8192]{2,1,0:T(8,128)} %get-tuple-element.56), channel_id=1, source_target_pairs={{0,24},{1,25},{2,26},{3,27},{4,28},{5,29},{6,30},{7,31},{8,0},{9,1... | collective-permute-start | bytes 3145736 | tf_op jit(solution)/shard_map/ppermute | solution.py:239
  179.2 38.9 %collective-permute-done.10 = f32[4,8,8192]{2,1,0:T(8,128)S(1)} collective-permute-done((f32[4,8,8192]{2,1,0:T(8,128)}, f32[4,8,8192]{2,1,0:T(8,128)S(1)}, u32[]{:S(2)}, u32[]{:S(2)}) %collective-permute-start.10) | collective-permute-done | bytes 1048608 | tf_op jit(solution)/shard_map/ppermute | solution.py:238
  218.2 1.3 collective-permute-start.17
  219.4 2.3 collective-permute-done.9
  221.7 1.2 fusion.20
  223.0 0.9 collective-permute-start.12
  223.9 2.4 collective-permute-start.13
  226.3 0.1 collective-permute-start.14
  226.4 19.6 %collective-permute-done.17 = f32[4,8,8192]{2,1,0:T(8,128)S(1)} collective-permute-done((f32[4,8,8192]{2,1,0:T(8,128)}, f32[4,8,8192]{2,1,0:T(8,128)S(1)}, u32[]{:S(2)}, u32[]{:S(2)}) %collective-permute-start.17) | collective-permute-done | bytes 1048608 | tf_op jit(solution)/shard_map/ppermute | solution.py:239
  246.0 1.3 fusion.13
  247.3 0.1 collective-permute-start.18
  247.4 3.6 %collective-permute-start.19 = (f32[8,8192]{1,0:T(8,128)S(1)}, f32[8,8192]{1,0:T(8,128)S(1)}, u32[]{:S(2)}, u32[]{:S(2)}) collective-permute-start(f32[8,8192]{1,0:T(8,128)S(1)} %get-tuple-element.64), channel_id=1, source_target_pairs={{0,6},{1,7},{2,0},{3,1},{4,2},{5,3},{6,4},{7,5},{8,14},{9,15},{10,... | collective-permute-start | bytes 786440 | tf_op jit(solution)/shard_map/ppermute | solution.py:243
  251.0 0.5 collective-permute-done.12
  251.6 0.9 collective-permute-start.20
  252.4 2.9 %collective-permute-done.14 = f32[8,8192]{1,0:T(8,128)S(1)} collective-permute-done((f32[8,8192]{1,0:T(8,128)S(1)}, f32[8,8192]{1,0:T(8,128)S(1)}, u32[]{:S(2)}, u32[]{:S(2)}) %collective-permute-start.14) | collective-permute-done | bytes 262176 | tf_op jit(solution)/shard_map/ppermute | solution.py:242
  255.4 1.1 fusion.24
  256.5 5.9 %collective-permute-done.20 = f32[8,8192]{1,0:T(8,128)S(1)} collective-permute-done((f32[8,8192]{1,0:T(8,128)S(1)}, f32[8,8192]{1,0:T(8,128)S(1)}, u32[]{:S(2)}, u32[]{:S(2)}) %collective-permute-start.20) | collective-permute-done | bytes 262176 | tf_op jit(solution)/shard_map/ppermute | solution.py:243
  262.4 1.1 fusion.17
  263.5 0.2 conditional.1
  263.8 0.8 copy-done.3
  (40 shorter events, 0.2 us)
Async XLA Ops:
  6.5 84.9 %all-gather.3.cloned.1.call-start = ((), (), s32[]{:S(2)}) async-start(), calls=%async_computation.6 | async-start | bytes 8912896 | tf_op jit(solution)/shard_map/all_gather | solution.py:216
  16.1 66.3 %collective-permute-start = (f32[40,128,128]{2,1,0:T(8,128)}, f32[40,128,128]{2,1,0:T(8,128)}, u32[]{:S(2)}, u32[]{:S(2)}) collective-permute-start(f32[40,128,128]{2,1,0:T(8,128)} %get-tuple-element.47), channel_id=1, source_target_pairs={{0,32},{32,64},{64,96},{96,0},{1,33},{33,65},{65,97},{97,1},{2,34}... | collective-permute-start | bytes 7864328 | tf_op jit(solution)/shard_map/ppermute | solution.py:247
  17.8 64.6 %collective-permute-start.1 = (f32[40,128,128]{2,1,0:T(8,128)}, f32[40,128,128]{2,1,0:T(8,128)S(1)}, u32[]{:S(2)}, u32[]{:S(2)}) collective-permute-start(f32[40,128,128]{2,1,0:T(8,128)} %get-tuple-element.48), channel_id=1, source_target_pairs={{0,96},{32,0},{64,32},{96,64},{1,97},{33,1},{65,33},{97,65},{2,98}... | collective-permute-start | bytes 7864328 | tf_op jit(solution)/shard_map/ppermute | solution.py:247
  27.0 54.8 %all-to-all-start.3 = ((f32[128,1,41]{2,1,0:T(1,128)}), f32[128,1,41]{2,1,0:T(1,128)S(1)}, u32[]{:S(2)}, u32[]{:S(2)}) async-start(f32[128,1,41]{2,1,0:T(1,128)} %bitcast.13), calls=%async_computation.4 | async-start | bytes 131072 | tf_op jit(solution)/shard_map/all_to_all | solution.py:258
  36.9 50.6 %collective-permute-start.2 = (f32[40,128,128]{2,1,0:T(8,128)}, f32[40,128,128]{2,1,0:T(8,128)}, u32[]{:S(2)}, u32[]{:S(2)}) collective-permute-start(f32[40,128,128]{2,1,0:T(8,128)} %get-tuple-element.46.refs_3_), channel_id=1, source_target_pairs={{0,1},{1,0},{2,3},{3,2},{4,5},{5,4},{6,7},{7,6},{8,9},{9,8},{10,11... | collective-permute-start | bytes 7864328 | tf_op jit(solution)/shard_map/ppermute | solution.py:270
  82.4 4.4 %copy-start.6 = (s32[2,4,40]{2,1,0:T(4,128)S(1)}, s32[2,4,40]{2,1,0:T(4,128)}, u32[]{:S(2)}) copy-start(s32[2,4,40]{2,1,0:T(4,128)} %maximum_convert_fusion.refs_1_) | copy-start | bytes 3844
  82.4 5.3 %collective-permute-start.3 = (f32[40,128,128]{2,1,0:T(8,128)}, f32[40,128,128]{2,1,0:T(8,128)}, u32[]{:S(2)}, u32[]{:S(2)}) collective-permute-start(f32[40,128,128]{2,1,0:T(8,128)} %shard_map.59.refs_4_), channel_id=1, source_target_pairs={{0,1},{1,0},{2,3},{3,2},{4,5},{5,4},{6,7},{7,6},{8,9},{9,8},{10,11... | collective-permute-start | bytes 7864328 | tf_op jit(solution)/shard_map/ppermute | solution.py:270
  82.4 1.5 copy-start
  83.9 7.5 %collective-permute-start.4 = (f32[40,128,128]{2,1,0:T(8,128)}, f32[40,128,128]{2,1,0:T(8,128)}, u32[]{:S(2)}, u32[]{:S(2)}) collective-permute-start(f32[40,128,128]{2,1,0:T(8,128)} %shard_map.60.refs_5_), channel_id=1, source_target_pairs={{0,1},{1,0},{2,3},{3,2},{4,5},{5,4},{6,7},{7,6},{8,9},{9,8},{10,11... | collective-permute-start | bytes 7864328 | tf_op jit(solution)/shard_map/ppermute | solution.py:270
  84.4 46.5 %collective-permute-start.5 = (f32[30,128,128]{2,1,0:T(8,128)}, f32[30,128,128]{2,1,0:T(8,128)S(1)}, u32[]{:S(2)}, u32[]{:S(2)}) collective-permute-start(f32[30,128,128]{2,1,0:T(8,128)} %get-tuple-element.49), channel_id=1, source_target_pairs={{0,64},{32,96},{64,0},{96,32},{1,65},{33,97},{65,1},{97,33},{2,66}... | collective-permute-start | bytes 5898248 | tf_op jit(solution)/shard_map/ppermute | solution.py:249
  130.8 1.3 copy-start.1
  132.1 4.2 %collective-permute-start.6 = (f32[30,128,128]{2,1,0:T(8,128)}, f32[30,128,128]{2,1,0:T(8,128)S(1)}, u32[]{:S(2)}, u32[]{:S(2)}) collective-permute-start(f32[30,128,128]{2,1,0:T(8,128)} %shard_map.62.refs_4_), channel_id=1, source_target_pairs={{0,1},{1,0},{2,3},{3,2},{4,5},{5,4},{6,7},{7,6},{8,9},{9,8},{10,11... | collective-permute-start | bytes 5898248 | tf_op jit(solution)/shard_map/ppermute | solution.py:270
  132.1 22.6 %collective-permute-start.7 = (f32[10,128,128]{2,1,0:T(8,128)}, f32[10,128,128]{2,1,0:T(8,128)S(1)}, u32[]{:S(2)}, u32[]{:S(2)}) collective-permute-start(f32[10,128,128]{2,1,0:T(8,128)} %get-tuple-element.44), channel_id=1, source_target_pairs={{0,64},{32,96},{64,0},{96,32},{1,65},{33,97},{65,1},{97,33},{2,66}... | collective-permute-start | bytes 1966088 | tf_op jit(solution)/shard_map/ppermute | solution.py:249
  136.3 1.3 copy-start.4
  154.8 0.8 copy-start.2
  155.6 2.3 collective-permute-start.8
  157.9 0.9 copy-start.5
  169.8 93.7 %copy-start.7 = (s32[128,1]{0,1:T(1,128)S(1)}, s32[128,1]{0,1:T(1,128)}, u32[]{:S(2)}) copy-start(s32[128,1]{0,1:T(1,128)} %param.9) | copy-start | bytes 1540
  169.8 93.7 %copy-start.8 = (s32[128]{0:T(128)S(1)}, s32[128]{0:T(128)}, u32[]{:S(2)}) copy-start(s32[128]{0:T(128)} %param.11) | copy-start | bytes 1540
  169.8 93.7 %copy-start.9 = (s32[128]{0:T(128)S(1)}, s32[128]{0:T(128)}, u32[]{:S(2)}) copy-start(s32[128]{0:T(128)} %param.10) | copy-start | bytes 1540
  169.8 48.3 %collective-permute-start.10 = (f32[4,8,8192]{2,1,0:T(8,128)}, f32[4,8,8192]{2,1,0:T(8,128)S(1)}, u32[]{:S(2)}, u32[]{:S(2)}) collective-permute-start(f32[4,8,8192]{2,1,0:T(8,128)} %get-tuple-element.52), channel_id=1, source_target_pairs={{0,6},{1,7},{2,0},{3,1},{4,2},{5,3},{6,4},{7,5},{8,14},{9,15},{10,... | collective-permute-start | bytes 3145736 | tf_op jit(solution)/shard_map/ppermute | solution.py:238
  172.6 46.8 %collective-permute-start.11 = (f32[4,8,8192]{2,1,0:T(8,128)}, f32[4,8,8192]{2,1,0:T(8,128)S(1)}, u32[]{:S(2)}, u32[]{:S(2)}) collective-permute-start(f32[4,8,8192]{2,1,0:T(8,128)} %get-tuple-element.53), channel_id=1, source_target_pairs={{0,4},{1,5},{2,6},{3,7},{4,0},{5,1},{6,2},{7,3},{8,12},{9,13},{10,... | collective-permute-start | bytes 3145736 | tf_op jit(solution)/shard_map/ppermute | solution.py:238
  173.5 48.2 %collective-permute-start.9 = (f32[4,8,8192]{2,1,0:T(8,128)}, f32[4,8,8192]{2,1,0:T(8,128)S(1)}, u32[]{:S(2)}, u32[]{:S(2)}) collective-permute-start(f32[4,8,8192]{2,1,0:T(8,128)} %get-tuple-element.51), channel_id=1, source_target_pairs={{0,2},{1,3},{2,4},{3,5},{4,6},{5,7},{6,0},{7,1},{8,10},{9,11},{10,... | collective-permute-start | bytes 3145736 | tf_op jit(solution)/shard_map/ppermute | solution.py:238
  175.9 50.4 %collective-permute-start.15 = (f32[4,8,8192]{2,1,0:T(8,128)}, f32[4,8,8192]{2,1,0:T(8,128)S(1)}, u32[]{:S(2)}, u32[]{:S(2)}) collective-permute-start(f32[4,8,8192]{2,1,0:T(8,128)} %get-tuple-element.55), channel_id=1, source_target_pairs={{0,8},{1,9},{2,10},{3,11},{4,12},{5,13},{6,14},{7,15},{8,16},{9,17... | collective-permute-start | bytes 3145736 | tf_op jit(solution)/shard_map/ppermute | solution.py:239
  176.5 49.9 %collective-permute-start.16 = (f32[4,8,8192]{2,1,0:T(8,128)}, f32[4,8,8192]{2,1,0:T(8,128)S(1)}, u32[]{:S(2)}, u32[]{:S(2)}) collective-permute-start(f32[4,8,8192]{2,1,0:T(8,128)} %get-tuple-element.56), channel_id=1, source_target_pairs={{0,24},{1,25},{2,26},{3,27},{4,28},{5,29},{6,30},{7,31},{8,0},{9,1... | collective-permute-start | bytes 3145736 | tf_op jit(solution)/shard_map/ppermute | solution.py:239
  218.2 27.9 %collective-permute-start.17 = (f32[4,8,8192]{2,1,0:T(8,128)}, f32[4,8,8192]{2,1,0:T(8,128)S(1)}, u32[]{:S(2)}, u32[]{:S(2)}) collective-permute-start(f32[4,8,8192]{2,1,0:T(8,128)} %get-tuple-element.57), channel_id=1, source_target_pairs={{0,16},{1,17},{2,18},{3,19},{4,20},{5,21},{6,22},{7,23},{8,24},{9,... | collective-permute-start | bytes 3145736 | tf_op jit(solution)/shard_map/ppermute | solution.py:239
  223.0 28.6 %collective-permute-start.12 = (f32[8,8192]{1,0:T(8,128)S(1)}, f32[8,8192]{1,0:T(8,128)S(1)}, u32[]{:S(2)}, u32[]{:S(2)}) collective-permute-start(f32[8,8192]{1,0:T(8,128)S(1)} %get-tuple-element.59), channel_id=1, source_target_pairs={{0,8},{1,9},{2,10},{3,11},{4,12},{5,13},{6,14},{7,15},{8,16},{9,17... | collective-permute-start | bytes 786440 | tf_op jit(solution)/shard_map/ppermute | solution.py:242
  223.9 28.6 %collective-permute-start.13 = (f32[8,8192]{1,0:T(8,128)S(1)}, f32[8,8192]{1,0:T(8,128)S(1)}, u32[]{:S(2)}, u32[]{:S(2)}) collective-permute-start(f32[8,8192]{1,0:T(8,128)S(1)} %get-tuple-element.61), channel_id=1, source_target_pairs={{0,24},{1,25},{2,26},{3,27},{4,28},{5,29},{6,30},{7,31},{8,0},{9,1... | collective-permute-start | bytes 786440 | tf_op jit(solution)/shard_map/ppermute | solution.py:242
  226.3 29.1 %collective-permute-start.14 = (f32[8,8192]{1,0:T(8,128)S(1)}, f32[8,8192]{1,0:T(8,128)S(1)}, u32[]{:S(2)}, u32[]{:S(2)}) collective-permute-start(f32[8,8192]{1,0:T(8,128)S(1)} %get-tuple-element.60), channel_id=1, source_target_pairs={{0,16},{1,17},{2,18},{3,19},{4,20},{5,21},{6,22},{7,23},{8,24},{9,... | collective-permute-start | bytes 786440 | tf_op jit(solution)/shard_map/ppermute | solution.py:242
  247.3 9.1 %collective-permute-start.18 = (f32[8,8192]{1,0:T(8,128)S(1)}, f32[8,8192]{1,0:T(8,128)S(1)}, u32[]{:S(2)}, u32[]{:S(2)}) collective-permute-start(f32[8,8192]{1,0:T(8,128)S(1)} %get-tuple-element.62), channel_id=1, source_target_pairs={{0,2},{1,3},{2,4},{3,5},{4,6},{5,7},{6,0},{7,1},{8,10},{9,11},{10,... | collective-permute-start | bytes 786440 | tf_op jit(solution)/shard_map/ppermute | solution.py:243
  247.4 9.0 %collective-permute-start.19 = (f32[8,8192]{1,0:T(8,128)S(1)}, f32[8,8192]{1,0:T(8,128)S(1)}, u32[]{:S(2)}, u32[]{:S(2)}) collective-permute-start(f32[8,8192]{1,0:T(8,128)S(1)} %get-tuple-element.64), channel_id=1, source_target_pairs={{0,6},{1,7},{2,0},{3,1},{4,2},{5,3},{6,4},{7,5},{8,14},{9,15},{10,... | collective-permute-start | bytes 786440 | tf_op jit(solution)/shard_map/ppermute | solution.py:243
  251.6 10.8 %collective-permute-start.20 = (f32[8,8192]{1,0:T(8,128)S(1)}, f32[8,8192]{1,0:T(8,128)S(1)}, u32[]{:S(2)}, u32[]{:S(2)}) collective-permute-start(f32[8,8192]{1,0:T(8,128)S(1)} %get-tuple-element.63), channel_id=1, source_target_pairs={{0,4},{1,5},{2,6},{3,7},{4,0},{5,1},{6,2},{7,3},{8,12},{9,13},{10,... | collective-permute-start | bytes 786440 | tf_op jit(solution)/shard_map/ppermute | solution.py:243
  263.8 0.8 copy-start.3
Sparse Core Ops, SparseCore 0:
  9.5 73.4 all-gather.2
